TPU v7x, 32 devices: a whole 2x2x4 slice. The times are simulated.
32 devices in a mesh: dp: 8 (over z, y), tensor: 4 (over x, core).
Axes of the slice: x: 2, y: 2, z: 4, core: 2. Of those that a mesh axis runs over, the one named last changes fastest.
Arguments:
- tokens: bfloat16 [24, 1024, 1536], P('dp'), may hold values from -6 to 6
- cotangent: bfloat16 [24, 1024, 1536], P('dp'), may hold values from -6 to 6
- norm_gain: float32 [1536], replicated, may hold values from 0.8 to 6, as said below
- w_zx: float32 [1536, 2, 3072], P('dp', None, 'tensor'), may hold values from -0.15625 to 0.15625
- state_proj_weight: float32 [1536, 256], P('dp'), may hold values from -0.15625 to 0.15625
- step_weight: float32 [1536, 48], P('dp', 'tensor'), may hold values from -0.078125 to 0.078125
- exit_coefficient_matrix: float32 [3072, 1536], P('tensor', 'dp'), may hold values from -0.0546875 to 0.0546875
- x_params: float32 [6, 3072], P(None, 'tensor')
- bc_params: float32 [5, 256], replicated
- head_params: float32 [3, 48], P(None, 'tensor'), may hold values from -9.3 to 2.8, as said below
- zx_moment: float32 [1536, 2, 3072], P('dp', None, 'tensor'), may hold values from -448 to 448
- bc_moment: float32 [1536, 256], P('dp'), may hold values from -448 to 448
- dt_moment: float32 [1536, 48], P('dp', 'tensor'), may hold values from -112 to 112
- out_moment: float32 [3072, 1536], P('tensor', 'dp'), may hold values from -448 to 448
- gain_moment: float32 [1536], replicated, may hold values from -448 to 448
- xpar_moment: float32 [6, 3072], P(None, 'tensor'), may hold values from -448 to 448
- bcpar_moment: float32 [5, 256], replicated, may hold values from -448 to 448
- head_moment: float32 [3, 48], P(None, 'tensor'), may hold values from -448 to 448
Outputs:
- result: bfloat16 [24, 1024, 1536], P('dp', None, 'tensor')
- input_grad: float32 [24, 1024, 1536], P('dp', None, 'tensor')
- zx_moment_new: float32 [1536, 2, 3072], P('dp', None, 'tensor')
- zx_new: float32 [1536, 2, 3072], P('dp', None, 'tensor')
- bc_moment_new: float32 [1536, 256], P('dp')
- bc_new: float32 [1536, 256], P('dp')
- dt_moment_new: float32 [1536, 48], P('dp', 'tensor')
- dt_new: float32 [1536, 48], P('dp', 'tensor')
- out_moment_new: float32 [3072, 1536], P('tensor', 'dp')
- out_new: float32 [3072, 1536], P('tensor', 'dp')
- gain_moment_new: float32 [1536], replicated
- gain_new: float32 [1536], replicated
- xpar_moment_new: float32 [6, 3072], P(None, 'tensor')
- xpar_new: float32 [6, 3072], P(None, 'tensor')
- bcpar_moment_new: float32 [5, 256], replicated
- bcpar_new: float32 [5, 256], replicated
- head_moment_new: float32 [3, 48], P(None, 'tensor')
- head_new: float32 [3, 48], P(None, 'tensor')
Inputs may be any that keep to these rules, and one draw needn't show every extreme that they name: `norm_gain`: positive, varying along the features. `head_params`: row 0 is the log of a positive decay rate, row 1 a step bias, row 2 a positive skip gain.
All inputs are finite; a program needn't handle non-finite values.
Results may differ from a plain program's by a relative error of at most 0.012.
The roundings to bfloat16 on the way count: a program that leaves them out, or rounds other values in their place, can miss the bound.
Values may be sent and summed in bfloat16 or wider, within the bound.
No kernel may reach another device: no remote copies, remote signals or barrier semaphores. Data moves between devices by JAX's collectives and lax.ppermute only.
A program may use at most 320 MiB of HBM per device.

v0:
```python
import jax
import jax.numpy as jnp
from jax import lax
from jax.sharding import PartitionSpec as P

GROUP = 256
INNER = 3072


finest_arithmetic_mode = lax.Precision.HIGHEST
high_split = lax.Precision.HIGH
single_pass = lax.Precision.DEFAULT
norm_eps = 1e-05
poly_first = 3.4445
poly_second = -4.775
poly_third = 2.0315
momentum_rate = 0.95
matrix_rate = 0.5
weight_decay = 0.1
small_rate = 0.0025


def conv_silu(signal, conv_taps, conv_bias):
    width_taps = conv_taps.shape[0]
    length = signal.shape[1]
    padded = jnp.pad(signal, ((0, 0), (width_taps - 1, 0), (0, 0)))
    summed = conv_bias + sum(
        (conv_taps[offset] * padded[:, offset : offset + length] for offset in range(width_taps))
    )
    return jax.nn.silu(summed)


def block_step(state_carry, pieces, skip_gain):
    block_x, block_b, block_c, block_decay, block_size = pieces
    span = block_x.shape[1]
    running = jnp.cumsum(block_decay, axis=1)
    by_head = jnp.swapaxes(running, 1, 2)
    log_gap = by_head[:, :, :, None] - by_head[:, :, None, :]
    later = lax.broadcasted_iota(jnp.int32, (span, span), 0)
    earlier = lax.broadcasted_iota(jnp.int32, (span, span), 1)
    causal = later >= earlier
    kernel = jnp.where(causal, jnp.exp(jnp.where(causal, log_gap, 0.0)), 0.0)
    scores = jnp.einsum("stn,sun->stu", block_c, block_b, precision=single_pass)
    weighted = kernel * scores[:, None]
    scaled_x = block_x * block_size[..., None]
    inside = jnp.einsum("shtu,suhp->sthp", weighted, scaled_x, precision=high_split)
    carried = (
        jnp.einsum("stn,shpn->sthp", block_c, state_carry, precision=high_split)
        * jnp.exp(running)[..., None]
    )
    tail_decay = jnp.exp(running[:, -1:, :] - running)
    renewed = state_carry * jnp.exp(running[:, -1, :])[:, :, None, None] + jnp.einsum(
        "suhp,sun->shpn", scaled_x * tail_decay[..., None], block_b, precision=high_split
    )
    return (renewed, inside + carried + skip_gain[:, None] * block_x)


def mixer(conv_x, conv_bc, step_preactivation, head_params):
    sequences, length, inner_width = conv_x.shape
    head_count = head_params.shape[1]
    head_width = inner_width // head_count
    state_width = conv_bc.shape[2] // 2
    blocks = length // GROUP
    step_size = jax.nn.softplus(step_preactivation + head_params[1])
    log_decay = -step_size * jnp.exp(head_params[0])

    def to_blocks(array):
        shaped = array.reshape((sequences, blocks, length // blocks) + array.shape[2:])
        return jnp.moveaxis(shaped, 1, 0)

    pieces = (
        to_blocks(conv_x.reshape(sequences, length, head_count, head_width)),
        to_blocks(conv_bc[:, :, :state_width]),
        to_blocks(conv_bc[:, :, state_width:]),
        to_blocks(log_decay),
        to_blocks(step_size),
    )
    start_state = jnp.zeros((sequences, head_count, head_width, state_width), jnp.float32)
    stepper = jax.checkpoint(
        lambda state_carry, block_pieces: block_step(state_carry, block_pieces, head_params[2])
    )
    final_state, outputs = lax.scan(stepper, start_state, pieces)
    return jnp.moveaxis(outputs, 0, 1).reshape(sequences, length, inner_width)


def to_matrices(zx_in, bc_in, dt_in, out_in, head_width):
    row_count = zx_in.shape[0]
    head_count = dt_in.shape[1]
    state_width = bc_in.shape[1] // 2
    zx_mats = jnp.transpose(
        zx_in.reshape(row_count, 2, head_count, head_width), (1, 2, 0, 3)
    ).reshape(2 * head_count, row_count, head_width)
    out_mats = jnp.transpose(out_in.reshape(head_count, head_width, row_count), (0, 2, 1))
    head_mats = jnp.concatenate([zx_mats, out_mats], axis=0)
    bc_mats = jnp.transpose(bc_in.reshape(row_count, 2, state_width), (1, 0, 2))
    dt_mats = jnp.transpose(dt_in, (1, 0))[:, :, None]
    return (head_mats, bc_mats, dt_mats)


def from_matrices(head_mats, bc_mats, dt_mats):
    head_count = dt_mats.shape[0]
    row_count = head_mats.shape[1]
    head_width = head_mats.shape[2]
    zx_mats = head_mats[: 2 * head_count].reshape(2, head_count, row_count, head_width)
    zx_back = jnp.transpose(zx_mats, (2, 0, 1, 3)).reshape(row_count, 2, head_count * head_width)
    out_back = jnp.transpose(head_mats[2 * head_count :], (0, 2, 1)).reshape(
        head_count * head_width, row_count
    )
    bc_back = jnp.transpose(bc_mats, (1, 0, 2)).reshape(row_count, -1)
    dt_back = jnp.transpose(dt_mats[:, :, 0], (1, 0))
    return (zx_back, bc_back, dt_back, out_back)


def gram_of(square_array_operand):
    return jnp.einsum(
        "mri,mrj->mij", square_array_operand, square_array_operand, precision=finest_arithmetic_mode
    )


def newton_steps(mats, combine):
    gram_list = combine(tuple((gram_of(square_array_operand) for square_array_operand in mats)))
    scales = tuple(
        (1.0 / (jnp.sqrt(jnp.einsum("mii->m", gram_matrix)) + 1e-07) for gram_matrix in gram_list)
    )
    current = tuple(
        (
            square_array_operand * norm_scale[:, None, None]
            for square_array_operand, norm_scale in zip(mats, scales)
        )
    )
    gram_list = tuple(
        (
            gram_matrix * (norm_scale * norm_scale)[:, None, None]
            for gram_matrix, norm_scale in zip(gram_list, scales)
        )
    )
    for sweep_index in range(5):
        if sweep_index > 0:
            gram_list = combine(
                tuple((gram_of(square_array_operand) for square_array_operand in current))
            )
        current = tuple(
            (
                poly_first * square_array_operand
                + jnp.einsum(
                    "mri,mij->mrj",
                    square_array_operand,
                    poly_second * gram_matrix
                    + poly_third
                    * jnp.einsum(
                        "mij,mjk->mik", gram_matrix, gram_matrix, precision=finest_arithmetic_mode
                    ),
                    precision=finest_arithmetic_mode,
                )
                for square_array_operand, gram_matrix in zip(current, gram_list)
            )
        )
    return current


def unchanged(gram_list):
    return gram_list


def silu_slope(value):
    logistic = jax.nn.sigmoid(value)
    return logistic * (1.0 + value * (1.0 - logistic))


def rounded(value):
    return lax.optimization_barrier(value.astype(jnp.bfloat16)).astype(jnp.float32)


def local(
    tokens,
    cotangent,
    norm_gain,
    w_zx,
    state_proj_weight,
    step_weight,
    exit_coefficient_matrix,
    x_params,
    bc_params,
    head_params,
    zx_moment,
    bc_moment,
    dt_moment,
    out_moment,
    gain_moment,
    xpar_moment,
    bcpar_moment,
    head_moment,
):
    kwidth = bc_params.shape[0] - 1
    head_count = head_params.shape[1]
    head_width = x_params.shape[1] // head_count
    share_rows = w_zx.shape[0]
    model_width = tokens.shape[2]
    share_width = model_width // lax.axis_size("tensor")
    share_start = lax.axis_index("tensor") * share_width
    (
        gathered_gate_input_weight,
        gathered_state_proj,
        gathered_step_weight,
        assembled_exit_coefficients,
    ) = (
        lax.all_gather(w_zx.astype(jnp.bfloat16), "dp", axis=0, tiled=True),
        lax.all_gather(state_proj_weight.astype(jnp.bfloat16), "dp", axis=0, tiled=True),
        lax.all_gather(step_weight.astype(jnp.bfloat16), "dp", axis=0, tiled=True),
        lax.all_gather(exit_coefficient_matrix.astype(jnp.bfloat16), "dp", axis=1, tiled=True),
    )
    entering_token_vectors = tokens.astype(jnp.float32)
    inv_rms = lax.rsqrt(
        jnp.mean(entering_token_vectors * entering_token_vectors, axis=-1, keepdims=True) + norm_eps
    )
    normalized_input = (entering_token_vectors * inv_rms * norm_gain).astype(jnp.bfloat16)
    gate_preactivation = jnp.einsum(
        "gtc,cu->gtu",
        normalized_input,
        gathered_gate_input_weight[:, 0],
        preferred_element_type=jnp.float32,
    )
    convolve_input = jnp.einsum(
        "gtc,cu->gtu",
        normalized_input,
        gathered_gate_input_weight[:, 1],
        preferred_element_type=jnp.float32,
    )
    state_proj_preconv = jnp.einsum(
        "gmq,qp->gmp", normalized_input, gathered_state_proj, preferred_element_type=jnp.float32
    )
    step_preactivation = jnp.einsum(
        "bpj,jt->bpt", normalized_input, gathered_step_weight, preferred_element_type=jnp.float32
    )
    conv_x_full, conv_x_back = jax.vjp(
        conv_silu, convolve_input, x_params[:kwidth], x_params[kwidth]
    )
    conv_bc_full, conv_bc_back = jax.vjp(
        conv_silu, state_proj_preconv, bc_params[:kwidth], bc_params[kwidth]
    )
    conv_x = rounded(conv_x_full)
    conv_bc = rounded(conv_bc_full)
    mixed_y, mixer_back = jax.vjp(mixer, conv_x, conv_bc, step_preactivation, head_params)
    gate_act = jax.nn.silu(gate_preactivation)
    gated = mixed_y * gate_act
    squares = lax.psum(jnp.sum(gated * gated, axis=-1), "tensor")
    inverse = lax.rsqrt(squares / INNER + norm_eps)[..., None]
    gate_gain = x_params[kwidth + 1]
    blended_result_vectors = (gated * inverse * gate_gain).astype(jnp.bfloat16)
    partial_output = jnp.einsum(
        "gkt,to->gko",
        blended_result_vectors,
        assembled_exit_coefficients,
        preferred_element_type=jnp.float32,
    )
    out_share = lax.psum_scatter(partial_output, "tensor", scatter_dimension=2, tiled=True)
    inputs_share = lax.dynamic_slice_in_dim(entering_token_vectors, share_start, share_width, 2)
    result = (inputs_share + out_share).astype(jnp.bfloat16)
    mixed_output_gradient = jnp.einsum(
        "yua,va->yuv", cotangent, assembled_exit_coefficients, preferred_element_type=jnp.float32
    )
    output_gradient = jnp.einsum(
        "vyw,vyk->wk", blended_result_vectors, cotangent, preferred_element_type=jnp.float32
    )
    scaled = mixed_output_gradient * gate_gain
    gate_inner = lax.psum(jnp.sum(scaled * gated, axis=-1), "tensor")
    grad_gated = inverse * scaled - gated * inverse**3 * (gate_inner / INNER)[..., None]
    grad_gate_gain = jnp.sum(mixed_output_gradient * gated * inverse, axis=(0, 1))
    grad_y = grad_gated * gate_act
    gate_gradient = (grad_gated * mixed_y * silu_slope(gate_preactivation)).astype(jnp.bfloat16)
    grad_conv_x, grad_bc_part, grad_delta_full, grad_head = mixer_back(grad_y)
    step_size_gradient = grad_delta_full.astype(jnp.bfloat16)
    grad_conv_bc = lax.psum(grad_bc_part, "tensor")
    grad_bc_full, grad_bc_taps, grad_bc_bias = conv_bc_back(grad_conv_bc)
    state_preconv_gradient = grad_bc_full.astype(jnp.bfloat16)
    grad_in_full, grad_x_taps, grad_x_bias = conv_x_back(grad_conv_x)
    convolve_input_gradient = grad_in_full.astype(jnp.bfloat16)
    partial_normed = jnp.einsum(
        "ypu,fu->ypf",
        gate_gradient,
        gathered_gate_input_weight[:, 0],
        preferred_element_type=jnp.float32,
    )
    partial_normed = partial_normed + jnp.einsum(
        "ypu,fu->ypf",
        convolve_input_gradient,
        gathered_gate_input_weight[:, 1],
        preferred_element_type=jnp.float32,
    )
    partial_normed = partial_normed + jnp.einsum(
        "tzv,av->tza", step_size_gradient, gathered_step_weight, preferred_element_type=jnp.float32
    )
    normed_share = lax.psum_scatter(partial_normed, "tensor", scatter_dimension=2, tiled=True)
    state_proj_rows = lax.dynamic_slice_in_dim(gathered_state_proj, share_start, share_width, 0)
    normed_share = normed_share + jnp.einsum(
        "bmr,ir->bmi", state_preconv_gradient, state_proj_rows, preferred_element_type=jnp.float32
    )
    gain_share = lax.dynamic_slice_in_dim(norm_gain, share_start, share_width, 0)
    weighted = normed_share * gain_share
    gain_grad_share = jnp.sum(normed_share * inputs_share * inv_rms, axis=(0, 1))
    gain_padded = lax.dynamic_update_slice_in_dim(
        jnp.zeros((model_width,), jnp.float32), gain_grad_share, share_start, 0
    )
    prenorm_inner, gain_grad = lax.psum(
        (jnp.sum(weighted * inputs_share, axis=-1), gain_padded), "tensor"
    )
    upstream_share = lax.dynamic_slice_in_dim(cotangent, share_start, share_width, 2).astype(
        jnp.float32
    )
    input_grad = (
        upstream_share
        + inv_rms * weighted
        - inputs_share * inv_rms**3 * (prenorm_inner / model_width)[..., None]
    )
    grad_zx = jnp.stack(
        [
            jnp.einsum(
                "mnt,mna->ta", normalized_input, gate_gradient, preferred_element_type=jnp.float32
            ),
            jnp.einsum(
                "mnt,mna->ta",
                normalized_input,
                convolve_input_gradient,
                preferred_element_type=jnp.float32,
            ),
        ],
        axis=1,
    )
    state_proj_gradient = jnp.einsum(
        "zfg,zfp->gp", normalized_input, state_preconv_gradient, preferred_element_type=jnp.float32
    )
    step_weight_gradient = jnp.einsum(
        "jax,jao->xo", normalized_input, step_size_gradient, preferred_element_type=jnp.float32
    )
    zx_share, bc_share, dt_share, out_grad_share = (
        lax.psum_scatter(grad_zx, "dp", scatter_dimension=0, tiled=True),
        lax.psum_scatter(state_proj_gradient, "dp", scatter_dimension=0, tiled=True),
        lax.psum_scatter(step_weight_gradient, "dp", scatter_dimension=0, tiled=True),
        lax.psum_scatter(output_gradient, "dp", scatter_dimension=1, tiled=True),
    )
    xpar_local = jnp.concatenate([grad_x_taps, grad_x_bias[None], grad_gate_gain[None]], axis=0)
    bcpar_local = jnp.concatenate([grad_bc_taps, grad_bc_bias[None]], axis=0)
    gain_g, xpar_g, bcpar_g, head_g = lax.psum(
        (gain_grad, xpar_local, bcpar_local, grad_head), "dp"
    )
    zx_m = momentum_rate * zx_moment + zx_share
    bc_m = momentum_rate * bc_moment + bc_share
    dt_m = momentum_rate * dt_moment + dt_share
    out_m = momentum_rate * out_moment + out_grad_share
    zx_input = zx_share + momentum_rate * zx_m
    bc_input = bc_share + momentum_rate * bc_m
    dt_input = dt_share + momentum_rate * dt_m
    out_input = out_grad_share + momentum_rate * out_m
    head_mats, local_bc_mats, local_dt_mats = to_matrices(
        zx_input, bc_input, dt_input, out_input, head_width
    )
    mat_count = head_mats.shape[0]
    dp_count = lax.axis_size("dp")
    padded_count = -(-mat_count // dp_count) * dp_count
    filler = jnp.zeros((padded_count - mat_count,) + head_mats.shape[1:], jnp.float32)
    head_padded = jnp.concatenate([head_mats, filler], axis=0)
    owned = lax.all_to_all(head_padded, "dp", split_axis=0, concat_axis=1, tiled=True)
    owned_ortho = newton_steps((owned,), unchanged)[0]
    returned = lax.all_to_all(
        owned_ortho.astype(jnp.bfloat16), "dp", split_axis=1, concat_axis=0, tiled=True
    ).astype(owned_ortho.dtype)
    whole_bc, whole_dt = (
        lax.all_gather(bc_input.astype(jnp.bfloat16), "dp", axis=0, tiled=True).astype(
            bc_input.dtype
        ),
        lax.all_gather(dt_input.astype(jnp.bfloat16), "dp", axis=0, tiled=True).astype(
            dt_input.dtype
        ),
    )
    state_width = whole_bc.shape[1] // 2
    whole_bc_mats = jnp.transpose(whole_bc.reshape(whole_bc.shape[0], 2, state_width), (1, 0, 2))
    whole_dt_mats = jnp.transpose(whole_dt, (1, 0))[:, :, None]
    bc_done, dt_done = newton_steps((whole_bc_mats, whole_dt_mats), unchanged)
    row_start = lax.axis_index("dp") * share_rows
    bc_rows_o = lax.dynamic_slice_in_dim(bc_done, row_start, share_rows, 1)
    dt_rows_o = lax.dynamic_slice_in_dim(dt_done, row_start, share_rows, 1)
    zx_ortho, bc_ortho, dt_ortho, out_ortho = from_matrices(
        returned[:mat_count], bc_rows_o, dt_rows_o
    )
    shrink = 1.0 - matrix_rate * weight_decay
    zx_new = w_zx * shrink - matrix_rate * zx_ortho
    bc_new = state_proj_weight * shrink - matrix_rate * bc_ortho
    dt_new = step_weight * shrink - matrix_rate * dt_ortho
    out_new = exit_coefficient_matrix * shrink - matrix_rate * out_ortho
    gain_m = momentum_rate * gain_moment + gain_g
    xpar_m = momentum_rate * xpar_moment + xpar_g
    bcpar_m = momentum_rate * bcpar_moment + bcpar_g
    head_m = momentum_rate * head_moment + head_g
    gain_new = norm_gain - small_rate * (gain_g + momentum_rate * gain_m)
    xpar_new = x_params - small_rate * (xpar_g + momentum_rate * xpar_m)
    bcpar_new = bc_params - small_rate * (bcpar_g + momentum_rate * bcpar_m)
    head_new = head_params - small_rate * (head_g + momentum_rate * head_m)
    return (
        result,
        input_grad,
        zx_m,
        zx_new,
        bc_m,
        bc_new,
        dt_m,
        dt_new,
        out_m,
        out_new,
        gain_m,
        gain_new,
        xpar_m,
        xpar_new,
        bcpar_m,
        bcpar_new,
        head_m,
        head_new,
    )


def solution(mesh):
    return jax.shard_map(
        local,
        mesh=mesh,
        in_specs=(
            P("dp", None, None),
            P("dp", None, None),
            P(),
            P("dp", None, "tensor"),
            P("dp", None),
            P("dp", "tensor"),
            P("tensor", "dp"),
            P(None, "tensor"),
            P(),
            P(None, "tensor"),
            P("dp", None, "tensor"),
            P("dp", None),
            P("dp", "tensor"),
            P("tensor", "dp"),
            P(),
            P(None, "tensor"),
            P(),
            P(None, "tensor"),
        ),
        out_specs=(
            P("dp", None, "tensor"),
            P("dp", None, "tensor"),
            P("dp", None, "tensor"),
            P("dp", None, "tensor"),
            P("dp", None),
            P("dp", None),
            P("dp", "tensor"),
            P("dp", "tensor"),
            P("tensor", "dp"),
            P("tensor", "dp"),
            P(),
            P(),
            P(None, "tensor"),
            P(None, "tensor"),
            P(),
            P(),
            P(None, "tensor"),
            P(None, "tensor"),
        ),
        check_vma=False,
    )
```

profile of v0, /device:TPU:0, one launch (start us, length us, event | category | flops | bytes accessed | tf_op | source)
XLA Modules:
  0.0 1572.8 jit_solution(792755686738785140)
XLA Ops:
  18.4 36.0 %all_gather.20 = bf16[1536,256]{1,0:T(8,128)(2,1)S(1)} all-gather(bf16[192,256]{1,0:T(8,128)(2,1)S(1)} %convert_element_type.79), channel_id=1, replica_groups=mesh['dp'=8,'tensor'=4] {'dp'}, dimensions={0}, use_global_device_ids=true | all-gather | bytes 884736 | tf_op jit(solution)/shard_map/all_gather | solution.py:208
  62.5 31.2 %all-gather = bf16[8,192,12]{1,2,0:T(8,128)(2,1)S(1)} all-gather(bf16[1,192,12]{1,2,0:T(8,128)(2,1)S(1)} %convert_bitcast_fusion), channel_id=1, replica_groups=mesh['dp'=8,'tensor'=4] {'dp'}, dimensions={0}, use_global_device_ids=true | all-gather | bytes 41472 | tf_op jit(solution)/shard_map/all_gather | solution.py:209
  159.7 102.2 %while.46 = (s32[]{:T(128)}, f32[3,12,64,128]{3,2,1,0:T(8,128)S(1)}, f32[4,3,256,12,64]{2,4,3,1,0:T(8,128)}, f32[4,3,12,64,128]{4,3,2,1,0:T(8,128)}, f32[4,3,256...) while((s32[]{:T(128)}, ...), condition=%wide.region_4.5_spmd.clone.clone, body=%wide.region_1.4_spmd.clone.clone.sunk | while | flops 1878500480 | bytes 24292592 | solution.py:82
  261.9 15.6 copy.351
  299.9 18.0 %multiply_reduce_fusion.14 = (f32[3,1024]{1,0:T(4,128)S(1)}, f32[3,1024,768]{2,1,0:T(8,128)}, f32[3,1024,768]{2,1,0:T(8,128)}) fusion(f32[3,1024,768]{2,1,0:T(8,128)} %copy.355, bf16[1536,2,768]{2,0,1:T(8,128)(2,1)} %all-gather.5.cloned.1.call-done, f32[1536]{0:T(1024)S(1)} %copy-done.89, f32[3,1024]{1,0:T(4,128)S(1)} %copy-done.53, ...), kind=kOutput, calls=%fused_computation.146 | convolution fusion | flops 7283143680 | bytes 40138752 | tf_op jit(solution)/shard_map/gtc,cu->gtu/dot_general | solution.py:217
  328.0 16.0 %multiply_reduce_fusion.8 = (f32[768]{0:T(1024)}, f32[3,1024]{1,0:T(4,128)S(1)}, f32[3,1024,768]{2,1,0:T(8,128)}) fusion(f32[3,1024,768]{2,1,0:T(8,128)} %get-tuple-element.969, f32[3,1024]{1,0:T(4,128)S(1)} %get-tuple-element.1011, f32[768]{0:T(1024)S(1)} %get-tuple-element.876, bf16[3,1024,1536]{2,1,0:T(8,128)(2,1)} %param.23, ...), kind=kOutput, calls=%fused_computation.137 | convolution fusion | flops 7261908992 | bytes 30701568 | tf_op jit(solution)/shard_map/yua,va->yuv/dot_general | solution.py:259
  354.1 19.5 %fusion.109 = (f32[3,1024,768]{2,1,0:T(8,128)}, bf16[3,1024,768]{2,1,0:T(8,128)(2,1)}) fusion(f32[3,1024]{1,0:T(4,128)S(1)} %broadcast_multiply_fusion.8, f32[3,1024,768]{2,1,0:T(8,128)} %get-tuple-element.969, f32[3,1024]{1,0:T(4,128)S(1)} %get-tuple-element.1010, f32[3,1024,768]{2,1,0:T(8,128)} %get-tuple-element.1022, f32[768]{0:T(1024)S(1)} %get-tuple-element.876, ...), kind=kLoop, calls=%fused_computation.207 | loop fusion | flops 40108032 | bytes 51944448 | tf_op jit(solution)/shard_map/mul | solution.py:269
  404.7 356.8 %while.45 = (s32[]{:T(128)}, f32[3,12]{1,0:T(4,128)}, f32[3,12,64,128]{3,2,1,0:T(8,128)}, f32[4,3,256,12,64]{2,4,3,1,0:T(8,128)}, f32[4,3,256,128]{3,2,1,0:T(8,1...) while((s32[]{:T(128)}, f32[3,12]{1,0:T(4,128)}, ...), condition=%wide.region_24.25_spmd.clone, body=%wide.region_10.24_spmd.clone.sunk | while | flops 4278437120 | bytes 129571592 | solution.py:82
  775.6 15.0 convolution_bitcast_fusion
  790.7 15.5 copy.361
  828.9 20.3 %multiply_reduce_fusion.12 = (f32[768]{0:T(1024)S(1)}, f32[768]{0:T(1024)S(1)}, f32[768]{0:T(1024)S(1)}, f32[768]{0:T(1024)S(1)}, f32[768]{0:T(1024)S(1)}, /*index=5*/f32[3,1024,768]{2,1,0:T(8,128)S(1)}) fusion(f32[3,1024,768]{2,1,0:T(8,128)} %copy-done.9, f32[3,1024,768]{2,1,0:T(8,128)} %get-tuple-element.973, f32[3,1024,768]{2,1,0:T(8,128)} %copy.362), kind=kLoop, calls=%fused_computation.141 | loop fusion | flops 42463488 | bytes 37764096 | tf_op jit(solution)/shard_map/transpose(jvp())/reduce_sum | solution.py:28
  849.3 14.8 broadcast_multiply_fusion
  864.1 13.3 fusion.94
  903.7 14.8 fusion.104
  935.0 14.4 fusion.106
  949.3 20.6 %add_add_fusion = f32[3,1024,1536]{2,1,0:T(8,128)} fusion(f32[3,1024,1536]{2,1,0:T(8,128)} %fusion.106, f32[3,1024,1536]{2,1,0:T(8,128)} %fusion.104, bf16[1536,12,1]{0,1,2:T(8,128)(2,1)S(1)} %copy-done.50, bf16[3,1024,12]{1,2,0:T(8,128)(2,1)S(1)} %get-tuple-element.951), kind=kOutput, calls=%fused_computation.126 | convolution fusion | flops 122683392 | bytes 56733696 | tf_op jit(solution)/shard_map/tzv,av->tza/dot_general | solution.py:290
  971.6 14.5 fusion.102
  1005.3 31.2 %all-gather.1 = bf16[8,192,12]{1,2,0:T(8,128)(2,1)S(1)} all-gather(bf16[1,192,12]{1,2,0:T(8,128)(2,1)S(1)} %get-tuple-element.958), channel_id=1, replica_groups=mesh['dp'=8,'tensor'=4] {'dp'}, dimensions={0}, use_global_device_ids=true | all-gather | bytes 41472 | tf_op jit(solution)/shard_map/all_gather | solution.py:371
  1040.6 126.2 %reduce-scatter.13.cloned.1.call-done = f32[192,2,768]{2,0,1:T(8,128)} async-done(((f32[1536,2,768]{2,0,1:T(8,128)}), f32[192,2,768]{2,0,1:T(8,128)}) %reduce-scatter.13.cloned.1.call-update) | async-done | bytes 1179664 | tf_op jit(solution)/shard_map/reduce_scatter | solution.py:336
  1177.9 95.2 %reduce-scatter.17.cloned.1.call-done = f32[192,256]{1,0:T(8,128)} async-done(((f32[1536,256]{1,0:T(8,128)}), f32[192,256]{1,0:T(8,128)}) %reduce-scatter.17.cloned.1.call-update) | async-done | bytes 196624 | tf_op jit(solution)/shard_map/reduce_scatter | solution.py:337
  1274.7 32.4 %all_gather.22 = bf16[1536,256]{1,0:T(8,128)(2,1)S(1)} all-gather(bf16[192,256]{1,0:T(8,128)(2,1)S(1)} %get-tuple-element.962), channel_id=1, replica_groups=mesh['dp'=8,'tensor'=4] {'dp'}, dimensions={0}, use_global_device_ids=true | all-gather | bytes 884736 | tf_op jit(solution)/shard_map/all_gather | solution.py:368
  1398.4 15.6 reduce-scatter.11.cloned.1.call-done
  1430.8 37.7 %all-reduce.25 = (f32[1536]{0:T(1024)S(1)}, f32[6,768]{1,0:T(8,128)S(1)}, f32[5,256]{1,0:T(8,128)S(1)}, f32[3,12]{1,0:T(4,128)S(1)}) all-reduce(f32[1536]{0:T(1024)S(1)} %get-tuple-element.941, f32[6,768]{1,0:T(8,128)S(1)} %copy-done.55, f32[5,256]{1,0:T(8,128)S(1)} %copy-done.77, ...), channel_id=1, replica_groups=mesh['dp'=8,'tensor'=4] {'dp'}, use_global_device_ids=true, to_apply=%region_37.38 | all-reduce | flops 7460 | bytes 59680 | tf_op jit(solution)/shard_map/psum | solution.py:343
  1470.9 85.4 %reduce-scatter.9.cloned.1.call-done = f32[3,1024,384]{2,1,0:T(8,128)} async-done(((f32[3,1024,1536]{2,1,0:T(8,128)}), f32[3,1024,384]{2,1,0:T(8,128)}) %reduce-scatter.9.cloned.1.call-update) | async-done | bytes 4718608 | tf_op jit(solution)/shard_map/reduce_scatter | solution.py:256
  (892 shorter events, 841.4 us)
Async XLA Ops:
  7.2 97.9 %all-gather.5.cloned.1.call-start = ((), (), s32[]{:S(2)}) async-start(), calls=%async_computation.8 | async-start | bytes 5308416 | tf_op jit(solution)/shard_map/all_gather | solution.py:207
  9.4 318.6 %all-gather.7.cloned.1.call-start = ((), (), s32[]{:S(2)}) async-start(), calls=%async_computation.9 | async-start | bytes 2654208 | tf_op jit(solution)/shard_map/all_gather | solution.py:210
  11.3 907.2 %all-reduce.29.cloned.1.call-start = ((), (), s32[]{:S(2)}) async-start(), calls=%async_computation.12 | async-start | bytes 6291456 | tf_op jit(solution)/shard_map/psum | solution.py:273
  18.4 86.7 %copy-start.52 = (f32[3,1024]{1,0:T(4,128)}, f32[3,1024]{1,0:T(4,128)S(1)}, u32[]{:S(2)}) copy-start(f32[3,1024]{1,0:T(4,128)S(1)} %get-tuple-element.1009) | copy-start | bytes 36868
  100.9 253.2 %copy-start.82 = (f32[768]{0:T(1024)}, f32[768]{0:T(1024)S(1)}, u32[]{:S(2)}) copy-start(f32[768]{0:T(1024)S(1)} %get-tuple-element.876) | copy-start | bytes 9220
  765.4 238.3 %reduce-scatter.19.cloned.1.call-start = ((), (), s32[]{:S(2)}) async-start(), calls=%async_computation.16 | async-start | bytes 884736
  775.5 262.8 %reduce-scatter.15.cloned.1.call-start = ((), (), s32[]{:S(2)}) async-start(), calls=%async_computation.14 | async-start | bytes 5308416 | tf_op jit(solution)/shard_map/reduce_scatter | solution.py:339
  790.6 376.2 %reduce-scatter.13.cloned.1.call-start = ((), (), s32[]{:S(2)}) async-start(), calls=%async_computation.13 | async-start | bytes 10616832 | tf_op jit(solution)/shard_map/reduce_scatter | solution.py:336
  903.7 369.4 %reduce-scatter.17.cloned.1.call-start = ((), (), s32[]{:S(2)}) async-start(), calls=%async_computation.15 | async-start | bytes 1769472 | tf_op jit(solution)/shard_map/reduce_scatter | solution.py:337
  934.9 479.1 %reduce-scatter.11.cloned.1.call-start = ((), (), s32[]{:S(2)}) async-start(), calls=%async_computation.11 | async-start | bytes 23592960 | tf_op jit(solution)/shard_map/reduce_scatter | solution.py:293
  969.9 586.4 %reduce-scatter.9.cloned.1.call-start = ((), (), s32[]{:S(2)}) async-start(), calls=%async_computation.10 | async-start | bytes 23592960 | tf_op jit(solution)/shard_map/reduce_scatter | solution.py:256
  1172.6 100.4 %copy-start.51 = (f32[192,256]{1,0:T(8,128)S(1)}, f32[192,256]{1,0:T(8,128)}, u32[]{:S(2)}) copy-start(f32[192,256]{1,0:T(8,128)} %param.33) | copy-start | bytes 589828
  1172.6 134.5 %copy-start.87 = (pred[128,128]{1,0:T(8,128)(4,1)S(1)}, pred[128,128]{1,0:T(8,128)(4,1)}, u32[]{:S(2)}) copy-start(pred[128,128]{1,0:T(8,128)(4,1)} %iota_compare_fusion.2) | copy-start | bytes 49156
  1172.6 146.3 %all-to-all-start = ((f32[40,192,64]{1,2,0:T(8,128)}), f32[40,192,64]{1,2,0:T(8,128)}, u32[]{:S(2)}, u32[]{:S(2)}) async-start(f32[40,192,64]{1,2,0:T(8,128)} %maximum_maximum_fusion), calls=%async_computation.4 | async-start | bytes 5242880 | tf_op jit(solution)/shard_map/all_to_all | solution.py:362
  1357.2 22.9 %all-to-all-start.1 = ((bf16[8,2,30720]{2,1,0:T(2,128)(2,1)}), bf16[8,2,30720]{2,1,0:T(2,128)(2,1)}, u32[]{:S(2)}, u32[]{:S(2)}) async-start(bf16[8,2,30720]{2,1,0:T(2,128)(2,1)} %reshape.620), calls=%async_computation.5 | async-start | bytes 1966080 | tf_op jit(solution)/shard_map/all_to_all | solution.py:364
  1398.3 70.1 %copy-start.115 = (f32[3,12]{1,0:T(4,128)S(1)}, f32[3,12]{1,0:T(4,128)}, u32[]{:S(2)}) copy-start(f32[3,12]{1,0:T(4,128)} %param.39) | copy-start | bytes 436
  1398.3 70.7 %copy-start.80 = (f32[5,256]{1,0:T(8,128)S(1)}, f32[5,256]{1,0:T(8,128)}, u32[]{:S(2)}) copy-start(f32[5,256]{1,0:T(8,128)} %param.30) | copy-start | bytes 15364
  1398.4 70.7 %copy-start.101 = (f32[5,256]{1,0:T(8,128)S(1)}, f32[5,256]{1,0:T(8,128)}, u32[]{:S(2)}) copy-start(f32[5,256]{1,0:T(8,128)} %param.38) | copy-start | bytes 15364
  1398.4 71.3 %copy-start.91 = (f32[1536]{0:T(1024)S(1)}, f32[1536]{0:T(1024)}, u32[]{:S(2)}) copy-start(f32[1536]{0:T(1024)} %param.24) | copy-start | bytes 18436
  1398.4 71.3 %copy-start.102 = (f32[1536]{0:T(1024)S(1)}, f32[1536]{0:T(1024)}, u32[]{:S(2)}) copy-start(f32[1536]{0:T(1024)} %param.36) | copy-start | bytes 18436
  1398.4 71.9 %copy-start.57 = (f32[6,768]{1,0:T(8,128)S(1)}, f32[6,768]{1,0:T(8,128)}, u32[]{:S(2)}) copy-start(f32[6,768]{1,0:T(8,128)} %param.29) | copy-start | bytes 55300
  1398.4 71.9 %copy-start.78 = (f32[6,768]{1,0:T(8,128)S(1)}, f32[6,768]{1,0:T(8,128)}, u32[]{:S(2)}) copy-start(f32[6,768]{1,0:T(8,128)} %param.37) | copy-start | bytes 55300
  1398.4 157.9 %copy-start.61 = (f32[3,1024]{1,0:T(4,128)S(1)}, f32[3,1024]{1,0:T(4,128)}, u32[]{:S(2)}) copy-start(f32[3,1024]{1,0:T(4,128)} %get-tuple-element.1008) | copy-start | bytes 36868
  1398.4 157.9 %copy-start.81 = (f32[384]{0:T(512)S(1)}, f32[384]{0:T(512)}, u32[]{:S(2)}) copy-start(f32[384]{0:T(512)} %dynamic_slice.116) | copy-start | bytes 4612
  (206 other events, 1716.3 us)
Sparse Core Ops, SparseCore 0:
  10.8 91.0 all-gather.4
  104.6 50.2 all-gather.6
  765.5 69.6 all-reduce.28
  839.0 62.5 reduce-scatter.18
  905.5 94.2 reduce-scatter.14
  1003.7 163.1 reduce-scatter.12
  1170.7 102.3 reduce-scatter.16
  1275.6 138.3 reduce-scatter.10
  1416.8 139.4 reduce-scatter.8
where the time goes:
time: 1590 us; the launch traced here: 1570 us
  matrix products  419 us (26%)
  local copies, waits for them, and re-layouts  334 us (21%)
  waiting for transfers between devices  329 us (21%)
  other arithmetic  254 us (16%)
  blocking collectives  199 us (13%)
    reduce_scatter x1, waiting for transfers between devices, local(): lax.psum_scatter(grad_zx, 'dp', scatter_dimension=0, tiled=True)  126 us
    dot_general x12, matrix products, block_step(): jnp.einsum('shtu,suhp->sthp', weighted, scaled_x, precision=high_split)  103 us
    reduce_scatter x1, waiting for transfers between devices, local(): lax.psum_scatter(state_proj_gradient, 'dp', scatter_dimension=0, tiled=True)  95.2 us
    reduce_scatter x1, waiting for transfers between devices, local(): lax.psum_scatter(partial_output, 'tensor', scatter_dimension=2, tiled=True)  85.4 us
    another operation x42, other arithmetic  83.3 us
    another operation x78, local copies, waits for them, and re-layouts  63.3 us
    dot_general x16, matrix products, block_step(): jnp.einsum('stn,shpn->sthp', block_c, state_carry, precision=high_split)  50.4 us
    transpose x9, local copies, waits for them, and re-layouts, to_blocks(): return jnp.moveaxis(shaped, 1, 0)  41.7 us
  transfers between devices with their start and end apart: 11, of which 5 were waited for; matrix products, arithmetic and copies ran while one was open for 36% of the time, Pallas kernels for 0%

commit v1 on v0

v1 whole, which is shorter than its diff:
```python
import functools

import jax
import jax.numpy as jnp
from jax import lax
from jax.experimental import pallas as pl
from jax.experimental.pallas import tpu as pltpu
from jax.sharding import PartitionSpec as P

BF = jnp.bfloat16
F32 = jnp.float32
CHUNK = 128
LANES = 128
ROWS = 256
PIECE = 64
WIDE_ROWS = 512
VMEM_BYTES = 52 * 1024 * 1024

exact = lax.Precision.HIGHEST
norm_eps = 1e-05
poly_first = 3.4445
poly_second = -4.775
poly_third = 2.0315
momentum_rate = 0.95
matrix_rate = 0.5
weight_decay = 0.1
small_rate = 0.0025


def params(count):
    return pltpu.CompilerParams(
        dimension_semantics=("arbitrary",) * count, vmem_limit_bytes=VMEM_BYTES
    )


def cost(flops, moved, transcendentals=0):
    return pl.CostEstimate(
        flops=flops // 40, bytes_accessed=moved // 40, transcendentals=transcendentals // 40
    )


def sigmoid(value):
    return 0.5 * jnp.tanh(0.5 * value) + 0.5


def dot(left, right):
    return jnp.dot(left, right, preferred_element_type=F32)


def dot_nt(left, right):
    return lax.dot_general(left, right, (((1,), (1,)), ((), ())), preferred_element_type=F32)


def halves(value):
    high = value.astype(BF)
    low = (value - high.astype(F32)).astype(BF)
    return high, low


def spread_dot(value, spread):
    high, low = halves(value)
    return dot(jnp.concatenate([high, low], axis=1), spread)


def gather_dot(value, spread):
    high, low = halves(value)
    return dot_nt(high, spread) + dot_nt(low, spread)


def tri_dot(triangle, value):
    first = value.astype(BF)
    rest = value - first.astype(F32)
    second = rest.astype(BF)
    third = (rest - second.astype(F32)).astype(BF)
    return dot(triangle, first) + dot(triangle, second) + dot(triangle, third)


def flip(value):
    return value.astype(F32).T.astype(BF)


def row_fold(value):
    return value.reshape(-1, 8, value.shape[-1]).sum(axis=0)


def tiles_of(start, stop, step):
    return [(low, min(step, stop - low)) for low in range(start, stop, step)]


def iota(shape, axis):
    return lax.broadcasted_iota(jnp.int32, shape, axis)


def project_kernel(
    kwidth, normed, weight, taps, heads, conv_in, bc_pre, conv_x, conv_bc, step, cum, buffer
):
    inner = conv_in.shape[-1]
    states = bc_pre.shape[-1]
    rows = normed.shape[1]
    block = pl.program_id(1)

    @pl.when(block == 0)
    def _():
        buffer[0:8, :] = jnp.zeros((8, inner + states), F32)

    @pl.when(block > 0)
    def _():
        buffer[0:8, :] = buffer[rows : rows + 8, :]

    data = normed[0]
    for low, width in tiles_of(0, inner, 256) + tiles_of(inner, inner + states, 256):
        cols = slice(low, low + width)
        made = dot(data, weight[:, cols])
        buffer[8 : 8 + rows, cols] = made
        for top in range(0, rows, PIECE):
            for left in range(low, low + width, LANES):
                here = slice(left, left + LANES)
                kept = buffer[8 + top : 8 + top + PIECE, here]
                total = taps[kwidth : kwidth + 1, here] + taps[kwidth - 1 : kwidth, here] * kept
                for offset in range(kwidth - 1):
                    start = 9 - kwidth + offset + top
                    total = total + taps[offset : offset + 1, here] * (
                        buffer[start : start + PIECE, here]
                    )
                active = (total * sigmoid(total)).astype(BF)
                span = slice(top, top + PIECE)
                if left < inner:
                    conv_in[0, span, here] = kept.astype(BF)
                    conv_x[0, span, here] = active
                else:
                    own = slice(left - inner, left - inner + LANES)
                    bc_pre[0, span, own] = kept
                    conv_bc[0, span, own] = active
    delta = dot(data, weight[:, inner + states :]) + heads[1:2, :]
    size = jnp.maximum(delta, 0.0) + jnp.log1p(jnp.exp(-jnp.abs(delta)))
    decay = -size * jnp.exp(heads[0:1, :])
    step[0] = size
    lower = (iota((CHUNK, CHUNK), 0) >= iota((CHUNK, CHUNK), 1)).astype(F32).astype(BF)
    for low in range(0, rows, CHUNK):
        cum[0, low : low + CHUNK, :] = tri_dot(lower, decay[low : low + CHUNK, :])


def scan_kernel(conv_x, conv_bc, step, cum, spread2, skip, y, states, state):
    inner = conv_x.shape[-1]
    width = conv_bc.shape[-1] // 2
    state[...] = jnp.zeros_like(state)
    causal = iota((CHUNK, CHUNK), 0) >= iota((CHUNK, CHUNK), 1)
    first = iota((CHUNK, LANES), 1) < LANES // 2
    spread = spread2[...]

    def body(index, carry):
        rows = pl.ds(pl.multiple_of(index * CHUNK, CHUNK), CHUNK)
        value = conv_x[0, rows, :]
        b_part = conv_bc[0, rows, :width]
        c_part = conv_bc[0, rows, width:]
        running = cum[0, rows, :]
        size = step[0, rows, :]
        state_low = state[...].astype(BF)
        states[0, index] = state_low
        scores = dot_nt(c_part, b_part)
        carried = dot(c_part, state_low)
        grow = spread_dot(jnp.exp(running), spread)
        tail = spread_dot(size * jnp.exp(running[CHUNK - 1 : CHUNK, :] - running), spread)
        keys = (running - jnp.log(size)).T
        for pair in range(inner // LANES):
            cols = slice(pair * LANES, (pair + 1) * LANES)
            pair_x = value[:, cols]
            parts = []
            for head in (2 * pair, 2 * pair + 1):
                gap = running[:, head : head + 1] - keys[head : head + 1, :]
                kernel = jnp.where(causal, jnp.exp(gap) * scores, 0.0).astype(BF)
                parts.append(dot(kernel, pair_x))
            y[0, rows, cols] = (
                jnp.where(first, parts[0], parts[1])
                + carried[:, cols] * grow[:, cols]
                + skip[0:1, cols] * pair_x.astype(F32)
            )
        weighted = (value.astype(F32) * tail).astype(BF)
        state[...] = state[...] * grow[CHUNK - 1 : CHUNK, :] + dot(flip(b_part), weighted)
        return carry

    lax.fori_loop(0, conv_x.shape[1] // CHUNK, body, 0)


def gate_kernel(normed, cotangent, weight, y, gain, gate_pre, grad_mixed, stats):
    inner = y.shape[-1]
    rows = normed.shape[1]
    data = normed[0]
    upstream = cotangent[0]
    squares = [jnp.zeros((PIECE, LANES), F32) for _ in range(rows // PIECE)]
    products = [jnp.zeros((PIECE, LANES), F32) for _ in range(rows // PIECE)]
    for low, width in tiles_of(0, inner, 256):
        cols = slice(low, low + width)
        pre_all = dot(data, weight[:, cols])
        grad_all = dot(upstream, weight[:, inner + low : inner + low + width])
        gate_pre[0, :, cols] = pre_all.astype(BF)
        grad_mixed[0, :, cols] = grad_all.astype(BF)
        for piece in range(rows // PIECE):
            span = slice(piece * PIECE, (piece + 1) * PIECE)
            for left in range(0, width, LANES):
                here = slice(low + left, low + left + LANES)
                pre = pre_all[span, left : left + LANES]
                gated = y[0, span, here] * pre * sigmoid(pre)
                squares[piece] = squares[piece] + gated * gated
                products[piece] = products[piece] + (
                    grad_all[span, left : left + LANES] * gain[0:1, here] * gated
                )
    squares = jnp.concatenate(squares, axis=0)
    products = jnp.concatenate(products, axis=0)
    lane = iota((rows, LANES), 1)
    both = jnp.where(
        lane == 0,
        jnp.sum(squares, axis=1, keepdims=True),
        jnp.where(lane == 1, jnp.sum(products, axis=1, keepdims=True), 0.0),
    )
    stats[0] = both.T[0:8, :]


def mix_kernel(
    starts,
    y,
    gate_pre,
    grad_mixed,
    scales,
    gain,
    weight,
    mixed,
    grad_y,
    grad_gate,
    own_core,
    other_core,
    gain_sum,
):
    inner = y.shape[-1]
    rows = y.shape[1]

    @pl.when((pl.program_id(0) == 0) & (pl.program_id(1) == 0))
    def _():
        gain_sum[...] = jnp.zeros_like(gain_sum)

    by_row = scales[0].T
    inverse = by_row[:, 0:1]
    slope = by_row[:, 1:2]
    for low in range(0, inner, LANES):
        cols = slice(low, low + LANES)
        gain_here = gain[0:1, cols]
        folded = jnp.zeros((8, LANES), F32)
        for top in range(0, rows, PIECE):
            span = slice(top, top + PIECE)
            value = y[0, span, cols]
            pre = gate_pre[0, span, cols].astype(F32)
            upstream = grad_mixed[0, span, cols].astype(F32)
            logistic = sigmoid(pre)
            act = pre * logistic
            gated = value * act
            scaled = gated * inverse[span]
            folded = folded + row_fold(upstream * scaled)
            mixed[0, span, cols] = (scaled * gain_here).astype(BF)
            grad_gated = inverse[span] * (upstream * gain_here) - gated * slope[span]
            grad_y[0, span, cols] = (grad_gated * act).astype(BF)
            grad_gate[0, span, cols] = (
                grad_gated * value * (logistic * (1.0 + pre * (1.0 - logistic)))
            ).astype(BF)
        gain_sum[:, cols] += folded
    data = mixed[0]
    share = own_core.shape[-1]
    columns = own_core.shape[0]
    for part in range(2 * columns):
        rows = pl.ds(pl.multiple_of(starts[part], share), share)
        made = dot_nt(data, weight[rows, :]).astype(BF)
        if part < columns:
            own_core[part, 0] = made
        else:
            other_core[part - columns, 0] = made


def back_kernel(
    kwidth,
    conv_x,
    conv_bc,
    step,
    cum,
    grad_y,
    y,
    states,
    conv_in,
    taps,
    heads,
    spread1,
    spread2,
    skip,
    in_before,
    old_taps,
    old_heads,
    after_in,
    after_bc,
    after_delta,
    grad_in,
    grad_bc,
    grad_delta,
    tap_sums,
    head_sums,
    grad_state,
    back_buffer,
    in_buffer,
):
    inner = conv_x.shape[-1]
    width = conv_bc.shape[-1] // 2
    chunks = conv_x.shape[1] // CHUNK
    step_index = pl.program_id(0)
    first_block = step_index == pl.num_programs(0) - 1

    @pl.when(step_index == 0)
    def _():
        tap_sums[...] = old_taps[...]
        head_sums[...] = old_heads[...]
        grad_state[...] = jnp.zeros_like(grad_state)
        back_buffer[0:8, :] = jnp.zeros((8, inner), F32)

    anti = iota((CHUNK, CHUNK), 0) <= iota((CHUNK, CHUNK), 1)
    upper = anti.astype(F32).astype(BF)
    first = iota((CHUNK, LANES), 1) < LANES // 2
    rate = jnp.exp(heads[0:1, :])
    spread = spread2[...]
    gather = spread1[...]

    for index in reversed(range(chunks)):
        rows = slice(index * CHUNK, (index + 1) * CHUNK)
        value = conv_x[0, rows, :]
        b_part = conv_bc[0, rows, :width]
        c_part = conv_bc[0, rows, width:]
        running = cum[0, rows, :]
        size = step[0, rows, :]
        upstream = grad_y[0, rows, :]
        old_state = states[0, index]
        state_grad = grad_state[...]
        state_grad_low = state_grad.astype(BF)
        scores = dot_nt(b_part, c_part)
        reach = dot(b_part, state_grad_low)
        grow = spread_dot(jnp.exp(running), spread)
        tail = spread_dot(size * jnp.exp(running[CHUNK - 1 : CHUNK, :] - running), spread)
        grown = (upstream.astype(F32) * grow).astype(BF)
        weighted = (value.astype(F32) * tail).astype(BF)
        grad_c = dot_nt(grown, old_state)
        grad_b = dot_nt(weighted, state_grad_low)
        last_grow = grow[CHUNK - 1 : CHUNK, :]
        grad_state[...] = state_grad * last_grow + dot(flip(c_part), grown)
        kept = row_fold(old_state.astype(F32) * state_grad) * last_grow
        queries = running.T
        keys = running - jnp.log(size)
        score_grad = jnp.zeros((CHUNK, CHUNK), F32)
        flow_parts = []
        pull_parts = []
        end_parts = []
        if index > 0:
            in_buffer[0:16, :] = conv_in[0, index * CHUNK - 16 : index * CHUNK, :].astype(F32)
        else:
            in_buffer[0:16, :] = jnp.where(first_block, 0.0, in_before[0].astype(F32))
        in_buffer[16 : 16 + CHUNK, :] = conv_in[0, rows, :].astype(F32)
        back_buffer[CHUNK : CHUNK + 8, :] = back_buffer[0:8, :]
        for pair in range(inner // LANES):
            cols = slice(pair * LANES, (pair + 1) * LANES)
            pair_x = value[:, cols]
            pair_up = upstream[:, cols]
            parts = []
            for side in (0, 1):
                head = 2 * pair + side
                gap = queries[head : head + 1, :] - keys[:, head : head + 1]
                kernel = jnp.where(anti, jnp.exp(gap), 0.0)
                own_x = jnp.where(first if side == 0 else ~first, pair_x, jnp.zeros_like(pair_x))
                score_grad = score_grad + kernel * dot_nt(own_x, pair_up)
                parts.append(dot((kernel * scores).astype(BF), pair_up))
            x_wide = pair_x.astype(F32)
            up_wide = pair_up.astype(F32)
            far = reach[:, cols] * tail[:, cols]
            inside = jnp.where(first, parts[0], parts[1]) + far
            skip_row = skip[0:1, cols]
            pull = x_wide * inside
            pull_parts.append(pull)
            flow_parts.append(up_wide * (y[0, rows, cols] - skip_row * x_wide) - pull)
            end_parts.append(row_fold(x_wide * far) + kept[:, cols])
            grad_x = inside + skip_row * up_wide
            now = in_buffer[16 : 16 + CHUNK, cols]
            shifted = [
                in_buffer[17 - kwidth + offset : 17 - kwidth + offset + CHUNK, cols]
                for offset in range(kwidth - 1)
            ] + [now]
            total = taps[kwidth : kwidth + 1, cols]
            for offset in range(kwidth):
                total = total + taps[offset : offset + 1, cols] * shifted[offset]
            logistic = sigmoid(total)
            error = grad_x * (logistic * (1.0 + total * (1.0 - logistic)))
            back_buffer[0:CHUNK, cols] = error
            for offset in range(kwidth):
                tap_sums[8 * offset : 8 * offset + 8, cols] += row_fold(error * shifted[offset])
            tap_sums[8 * kwidth : 8 * kwidth + 8, cols] += row_fold(error)
            tap_sums[8 * kwidth + 8 : 8 * kwidth + 16, cols] += row_fold(x_wide * up_wide)
            moved = taps[kwidth - 1 : kwidth, cols] * error
            for offset in range(kwidth - 1):
                start = kwidth - 1 - offset
                moved = moved + (
                    taps[offset : offset + 1, cols] * back_buffer[start : start + CHUNK, cols]
                )
            grad_in[0, rows, cols] = moved.astype(BF)
        score_low = score_grad.astype(BF)
        grad_bc[0, rows, :width] = (grad_b + dot(score_low, c_part)).astype(BF)
        grad_bc[0, rows, width:] = (grad_c + dot(flip(score_grad), b_part)).astype(BF)
        flow = gather_dot(jnp.concatenate(flow_parts, axis=1), gather)
        pull = gather_dot(jnp.concatenate(pull_parts, axis=1), gather)
        ends = gather_dot(jnp.concatenate(end_parts, axis=1), gather)
        decay_grad = tri_dot(upper, flow) + jnp.sum(ends, axis=0, keepdims=True)
        size_grad = pull / jnp.maximum(size, 1e-37) - rate * decay_grad
        small = size * (1.0 - size * (0.5 - size * (1.0 / 6.0)))
        delta_grad = size_grad * jnp.where(size < 0.01, small, 1.0 - jnp.exp(-size))
        grad_delta[0, rows, :] = delta_grad.astype(BF)
        head_sums[0:8, :] += row_fold(decay_grad * (-size * rate))
        head_sums[8:16, :] += row_fold(delta_grad)


def join_kernel(
    starts, grad_gate, grad_in, grad_delta, gate_weight, in_weight, step_weight, own_core, other_core
):
    share = own_core.shape[-1]
    columns = own_core.shape[0]
    for part in range(2 * columns):
        rows = pl.ds(pl.multiple_of(starts[part], share), share)
        total = dot_nt(grad_gate[0], gate_weight[rows, :])
        total = total + dot_nt(grad_in[0], in_weight[rows, :])
        total = total + dot_nt(grad_delta[0], step_weight[rows, :])
        if part < columns:
            own_core[part, 0] = total.astype(BF)
        else:
            other_core[part - columns, 0] = total.astype(BF)


def bc_kernel(kwidth, summed, pre, taps, grad_delta, grad_small, tap_sums, before, later):
    length = pre.shape[1]
    width = pre.shape[2]

    @pl.when(pl.program_id(0) == 0)
    def _():
        tap_sums[...] = jnp.zeros_like(tap_sums)

    before[0:8, :] = jnp.zeros((8, width), F32)
    before[8 : 8 + length, :] = pre[0]
    later[length : length + 8, :] = jnp.zeros((8, width), F32)
    for left in range(0, width, LANES):
        here = slice(left, left + LANES)

        folds = [jnp.zeros((8, LANES), F32) for _ in range(kwidth + 1)]
        for top in range(0, length, PIECE):
            span = slice(top, top + PIECE)
            shifted = [
                before[top + 9 - kwidth + offset : top + 9 - kwidth + offset + PIECE, here]
                for offset in range(kwidth)
            ]
            total = taps[kwidth : kwidth + 1, here]
            for offset in range(kwidth):
                total = total + taps[offset : offset + 1, here] * shifted[offset]
            logistic = sigmoid(total)
            error = summed[0, span, here].astype(F32) * (
                logistic * (1.0 + total * (1.0 - logistic))
            )
            later[span, here] = error
            for offset in range(kwidth):
                folds[offset] = folds[offset] + row_fold(error * shifted[offset])
            folds[kwidth] = folds[kwidth] + row_fold(error)
        for offset in range(kwidth + 1):
            tap_sums[8 * offset : 8 * offset + 8, here] += folds[offset]
        for top in range(0, length, PIECE):
            moved = taps[kwidth - 1 : kwidth, here] * later[top : top + PIECE, here]
            for offset in range(kwidth - 1):
                start = top + kwidth - 1 - offset
                moved = moved + taps[offset : offset + 1, here] * later[start : start + PIECE, here]
            grad_small[0, top : top + PIECE, here] = moved.astype(BF)
    grad_small[0, :, width:] = grad_delta[0]


def block_mask():
    half = LANES // 2
    return (iota((LANES, LANES), 0) < half) == (iota((LANES, LANES), 1) < half)


def pair_pack(matrix):
    half = LANES // 2
    return jnp.where(iota((half, LANES), 1) < half, matrix[:half], matrix[half:])


def pair_unpack(unit):
    half = LANES // 2
    left = iota((half, LANES), 1) < half
    return jnp.concatenate([jnp.where(left, unit, 0.0), jnp.where(left, 0.0, unit)], axis=0)


def gram_kernel(slots, first, second, squares, units):
    half = LANES // 2
    pairs, wholes, single = slots
    units[...] = jnp.zeros_like(units)
    split = first.shape[1] // LANES
    for index in range(pairs + len(wholes)):
        source, at = (first, index) if index < split else (second, index - split)
        part = source[:, at * LANES : (at + 1) * LANES]
        made = jnp.dot(part.T, part, precision=exact, preferred_element_type=F32)
        if index < pairs:
            units[index] = pair_pack(made)
        else:
            slot = wholes[index - pairs]
            units[slot] = made[:half]
            units[slot + 1] = made[half:]
    units[single, 0:8, :] = squares[...]


def newton_kernel(parts, kinds, result):
    half = LANES // 2
    same = block_mask()
    eye = (iota((LANES, LANES), 0) == iota((LANES, LANES), 1)).astype(F32)
    low_row = iota((LANES, 1), 0) < half
    low_col = iota((1, LANES), 1) < half

    def mul(left, right):
        return jnp.dot(left, right, precision=exact, preferred_element_type=F32)

    count = result.shape[0]
    sums = []
    for index in range(count):
        total = parts[0, index]
        for source in range(1, parts.shape[0]):
            total = total + parts[source, index]
        sums.append(total)
    whole = kinds[0:1, :] > 0.5
    is_whole = whole[:, 0:1]
    grams = [pair_unpack(unit) for unit in sums]
    grams[0] = jnp.where(whole, jnp.concatenate(sums[:2], axis=0), grams[0])
    scales = []
    for index in range(count):
        diagonal = jnp.sum(grams[index] * eye, axis=0, keepdims=True)
        low_trace = jnp.sum(jnp.where(low_col, diagonal, 0.0), axis=1, keepdims=True)
        high_trace = jnp.sum(jnp.where(low_col, 0.0, diagonal), axis=1, keepdims=True)
        if index == 0:
            both = low_trace + high_trace
            low_trace = jnp.where(is_whole, both, low_trace)
            high_trace = jnp.where(is_whole, both, high_trace)
        low_scale = 1.0 / (jnp.sqrt(low_trace) + 1e-07)
        high_scale = 1.0 / (jnp.sqrt(high_trace) + 1e-07)
        scale_row = jnp.where(low_row, low_scale, high_scale)
        scale_col = jnp.where(low_col, low_scale, high_scale)
        grams[index] = grams[index] * scale_row * scale_col
        scales.append(scale_row)
    totals = [None] * count
    for sweep in range(5):
        squares = [mul(gram, gram) for gram in grams]
        factors = [
            poly_first * eye + poly_second * gram + poly_third * square
            for gram, square in zip(grams, squares)
        ]
        totals = [
            scale * factor if sweep == 0 else mul(total, factor)
            for scale, total, factor in zip(scales, totals, factors)
        ]
        if sweep < 4:
            halfway = [mul(factor, gram) for factor, gram in zip(factors, grams)]
            grams = [mul(left, factor) for left, factor in zip(halfway, factors)]
    for index in range(count):
        made = pair_pack(totals[index])
        if index < 2:
            here = totals[0][:half] if index == 0 else totals[0][half:]
            made = jnp.where(whole, here, made)
        length = sums[index]
        scale = 1.0 / (jnp.sqrt(length) + 1e-07)
        length = length * scale * scale
        for sweep in range(5):
            step = poly_first + length * (poly_second + poly_third * length)
            scale = scale * step
            length = length * step * step
        single = kinds[8 + index : 9 + index, :] > 0.5
        result[index] = jnp.where(single, scale, made).astype(BF)


def apply_kernel(slots, first, second, units, made):
    pairs, wholes, single = slots
    split = first.shape[1] // LANES
    for index in range(pairs + len(wholes)):
        source, at = (first, index) if index < split else (second, index - split)
        if index < pairs:
            factor = pair_unpack(units[index].astype(F32))
        else:
            slot = wholes[index - pairs]
            factor = jnp.concatenate([units[slot], units[slot + 1]], axis=0).astype(F32)
        made[:, index * LANES : (index + 1) * LANES] = jnp.dot(
            source[:, at * LANES : (at + 1) * LANES],
            factor,
            precision=exact,
            preferred_element_type=F32,
        )


def whole_call(kernel, shapes, *operands):
    return pl.pallas_call(
        kernel,
        out_shape=shapes,
        compiler_params=pltpu.CompilerParams(vmem_limit_bytes=VMEM_BYTES),
    )(*operands)


def seen(shape, dtype=F32):
    return jax.ShapeDtypeStruct(shape, dtype)


def by_rows(width, rows=WIDE_ROWS):
    return pl.BlockSpec((1, rows, width), lambda s, t: (s, t, 0))


def fixed(shape, count):
    if count == 2:
        return pl.BlockSpec(shape, lambda s, t: (0,) * len(shape))
    return pl.BlockSpec(shape, lambda s: (0,) * len(shape))


def pad_rows(array, rows=8):
    return jnp.pad(array, ((0, rows - array.shape[0]), (0, 0)))


def pad_cols(array, cols):
    return jnp.pad(array, ((0, 0), (0, cols - array.shape[1])))


def copy_to_all(array, axis):
    count = lax.axis_size(axis)
    return lax.all_to_all(
        jnp.broadcast_to(array, (count,) + array.shape), axis, split_axis=0, concat_axis=0, tiled=True
    )


def block_starts(share):
    columns = lax.axis_size("tensor") // 2
    me = lax.axis_index("tensor")
    order = (me // 2 + jnp.arange(columns)) % columns
    return (
        share * jnp.concatenate([2 * order + me % 2, 2 * order + 1 - me % 2])
    ).astype(jnp.int32)


def core_sums(own, arrived):
    kept = own[0].astype(F32) + arrived[0].astype(F32)
    leaving = [
        (own[shift].astype(F32) + arrived[shift].astype(F32)).astype(BF)
        for shift in range(1, own.shape[0])
    ]
    return kept, leaving


def core_phase(own, other):
    count = lax.axis_size("tensor")
    return core_sums(own, lax.ppermute(other, "tensor", [(i, i ^ 1) for i in range(count)]))


def column_sends(leaving):
    count = lax.axis_size("tensor")
    columns = count // 2
    return [
        lax.ppermute(
            sent,
            "tensor",
            [(i, ((i // 2 + shift) % columns) * 2 + i % 2) for i in range(count)],
        )
        for shift, sent in enumerate(leaving, 1)
    ]


def column_phase(kept, leaving):
    for moved in column_sends(leaving):
        kept = kept + moved.astype(F32)
    return kept


def tensor_sum(value):
    count = lax.axis_size("tensor")
    step = 1
    while step < count:
        value = value + lax.ppermute(value, "tensor", [(i, i ^ step) for i in range(count)])
        step *= 2
    return value


def after(value, *others):
    return lax.optimization_barrier((value,) + others)[0]


def tie(*values):
    return lax.optimization_barrier(values)


def gather_rows(shard):
    count = lax.axis_size("dp")
    if count != 8:
        return lax.all_gather(shard, "dp", axis=0, tiled=True), shard, shard
    rows = shard.shape[0]
    me = lax.axis_index("dp")
    z = me // 2
    y = me % 2
    result = jnp.zeros((9 * rows, shard.shape[1]), shard.dtype)
    swap = [(i, i ^ 1) for i in range(count)]

    def place(result, piece, z_from, y_from):
        there = (z_from >= 0) & (z_from < 4)
        start = jnp.where(there, (z_from * 2 + y_from) * rows, 8 * rows)
        return lax.dynamic_update_slice_in_dim(result, piece, start, 0)

    other = lax.ppermute(shard, "dp", swap)
    result = place(result, shard, z, y)
    up = down = shard
    for step in range(1, 4):
        up = lax.ppermute(
            up, "dp", [(2 * i + j, 2 * i + 2 + j) for i in range(step - 1, 3) for j in range(2)]
        )
        down = lax.ppermute(
            down, "dp", [(2 * i + j, 2 * i - 2 + j) for i in range(1, 5 - step) for j in range(2)]
        )
        result = place(place(result, up, z - step, y), down, z + step, y)
    leaving = jnp.concatenate(
        [
            lax.dynamic_slice_in_dim(result, ((z ^ k) * 2 + y) * rows, rows, 0)
            for k in range(1, 4)
        ],
        axis=0,
    )
    arrived = lax.ppermute(leaving, "dp", swap)
    result = place(result, other, z, 1 - y)
    for k in range(1, 4):
        result = place(result, arrived[(k - 1) * rows : k * rows], z ^ k, 1 - y)
    return result, up, down


def sum_parts(parts):
    count = lax.axis_size("dp")
    return parts.reshape(count, -1, parts.shape[1]).astype(F32).sum(axis=0)


def add_low(left, right):
    return (left.astype(F32) + right.astype(F32)).astype(BF)


def chip_total(value):
    count = lax.axis_size("tensor")
    half = value.shape[1] // 2
    arrived = lax.ppermute(value, "tensor", [(i, i ^ 1) for i in range(count)])
    start = lax.axis_index("tensor") % 2 * half
    return add_low(
        lax.dynamic_slice_in_dim(value, start, half, 1),
        lax.dynamic_slice_in_dim(arrived, start, half, 1),
    )


def column_total_sends(part):
    count = lax.axis_size("tensor")
    return lax.ppermute(part, "tensor", [(i, i ^ 2) for i in range(count)])


def finish_total(part, moved):
    count = lax.axis_size("tensor")
    part = add_low(part, moved)
    step = 4
    while step < count:
        part = add_low(part, lax.ppermute(part, "tensor", [(i, i ^ step) for i in range(count)]))
        step *= 2
    other = lax.ppermute(part, "tensor", [(i, i ^ 1) for i in range(count)])
    first = lax.axis_index("tensor") % 2 == 0
    return jnp.concatenate(
        [jnp.where(first, part, other), jnp.where(first, other, part)], axis=1
    )


def dp_sum(value):
    count = lax.axis_size("dp")
    step = 1
    while step < count:
        value = value + lax.ppermute(value, "dp", [(i, i ^ step) for i in range(count)])
        step *= 2
    return value


def gram_units(first, second, squares):
    dp = lax.axis_size("dp")
    half = LANES // 2
    pairs = (first.shape[1] + second.shape[1]) // LANES - 2
    each = max(2, -(-pairs // (dp - 2)))
    wholes = ((dp - 2) * each, (dp - 1) * each)
    single = wholes[0] + 2 if each > 2 else wholes[0] - each
    slots = (pairs, wholes, single)
    square_rows = pad_rows(pad_cols(squares[None], LANES))
    units = whole_call(
        functools.partial(gram_kernel, slots),
        seen((dp * each, half, LANES)),
        first,
        second,
        square_rows,
    )
    return units, slots


def orthogonal(first, second, units, slots, count):
    dp = lax.axis_size("dp")
    half = LANES // 2
    each = units.shape[0] // dp
    single = slots[2]
    parts = lax.all_to_all(units, "dp", split_axis=0, concat_axis=0, tiled=True)
    me = lax.axis_index("dp")
    kinds = jnp.concatenate(
        [
            jnp.broadcast_to((me >= dp - 2).astype(F32), (8, LANES)),
            jnp.broadcast_to(
                (me * each + jnp.arange(8) == single).astype(F32)[:, None], (8, LANES)
            ),
        ],
        axis=0,
    )
    factors = whole_call(
        newton_kernel, seen((each, half, LANES), BF), parts.reshape(dp, each, half, LANES), kinds
    )
    factors = copy_to_all(factors, "dp").reshape(dp * each, half, LANES)
    made = whole_call(
        functools.partial(apply_kernel, slots),
        seen((first.shape[0], first.shape[1] + second.shape[1])),
        first,
        second,
        factors,
    )
    return made, factors[single, 0, :count].astype(F32)


def local(
    tokens,
    cotangent,
    norm_gain,
    w_zx,
    state_proj_weight,
    step_weight,
    exit_coefficient_matrix,
    x_params,
    bc_params,
    head_params,
    zx_moment,
    bc_moment,
    dt_moment,
    out_moment,
    gain_moment,
    xpar_moment,
    bcpar_moment,
    head_moment,
):
    kwidth = bc_params.shape[0] - 1
    heads = head_params.shape[1]
    inner = x_params.shape[1]
    head_width = inner // heads
    states = bc_params.shape[1]
    seqs, length, model = tokens.shape
    tensor = lax.axis_size("tensor")
    tensor_index = lax.axis_index("tensor")
    share = model // tensor
    share_start = tensor_index * share
    whole_inner = inner * tensor
    blocks = length // ROWS
    wide_blocks = length // WIDE_ROWS
    chunks = length // CHUNK
    tokens_here = seqs * length

    first_weight, last_up, last_down = gather_rows(
        jnp.concatenate(
            [w_zx[:, 1, :], state_proj_weight, pad_cols(step_weight, LANES)], axis=1
        ).astype(BF)
    )
    second_part = jnp.concatenate([w_zx[:, 0, :], exit_coefficient_matrix.T], axis=1).astype(BF)
    second_weight = lax.all_gather(
        after(second_part, last_up, last_down), "dp", axis=0, tiled=True
    )
    wide = after(tokens, last_up, last_down, second_part).astype(F32)
    inv_rms = lax.rsqrt(jnp.mean(wide * wide, axis=-1, keepdims=True) + norm_eps)
    normed = lax.optimization_barrier((wide * inv_rms * norm_gain).astype(BF))
    any_spec = pl.BlockSpec(memory_space=pl.ANY)

    starts = block_starts(share)

    taps = pad_rows(jnp.concatenate([x_params[: kwidth + 1], bc_params], axis=1))
    head_rows = pad_rows(pad_cols(head_params, LANES))
    lane_head = jnp.arange(inner) // head_width
    spread1 = (jnp.arange(LANES)[:, None] == lane_head[None, :]).astype(BF)
    spread2 = jnp.concatenate([spread1, spread1], axis=0)
    skip_row = jnp.broadcast_to(jnp.repeat(head_params[2], head_width)[None], (8, inner))
    gain_row = jnp.broadcast_to(x_params[kwidth + 1][None], (8, inner))

    first_cols = first_weight.shape[1]
    conv_in, bc_pre, conv_x, conv_bc, step, cum = pl.pallas_call(
        functools.partial(project_kernel, kwidth),
        grid=(seqs, wide_blocks),
        in_specs=[
            by_rows(model),
            fixed((model, first_cols), 2),
            fixed((8, inner + states), 2),
            fixed((8, LANES), 2),
        ],
        out_specs=[
            by_rows(inner),
            by_rows(states),
            by_rows(inner),
            by_rows(states),
            by_rows(LANES),
            by_rows(LANES),
        ],
        out_shape=[
            seen((seqs, length, inner), BF),
            seen((seqs, length, states)),
            seen((seqs, length, inner), BF),
            seen((seqs, length, states), BF),
            seen((seqs, length, LANES)),
            seen((seqs, length, LANES)),
        ],
        scratch_shapes=[pltpu.VMEM((WIDE_ROWS + 8, inner + states), F32)],
        compiler_params=params(2),
        cost_estimate=cost(
            28 * 10**9, tokens_here * (model + 3 * inner) * 2
        ),
        name="project",
    )(normed, first_weight, taps, head_rows)

    def per_seq(width):
        return pl.BlockSpec((1, length, width), lambda s: (s, 0, 0))

    state_spec = pl.BlockSpec((1, chunks, states // 2, inner), lambda s: (s, 0, 0, 0))
    mixed_y, old_states = pl.pallas_call(
        scan_kernel,
        grid=(seqs,),
        in_specs=[
            per_seq(inner),
            per_seq(states),
            per_seq(LANES),
            per_seq(LANES),
            fixed((2 * LANES, inner), 1),
            fixed((8, inner), 1),
        ],
        out_specs=[per_seq(inner), state_spec],
        out_shape=[
            seen((seqs, length, inner)),
            seen((seqs, chunks, states // 2, inner), BF),
        ],
        scratch_shapes=[pltpu.VMEM((states // 2, inner), F32)],
        compiler_params=params(1),
        cost_estimate=cost(
            20 * 10**9, tokens_here * inner * 8, tokens_here * heads * CHUNK
        ),
        name="scan",
    )(conv_x, conv_bc, step, cum, spread2, skip_row)

    stats_spec = pl.BlockSpec((1, 8, WIDE_ROWS), lambda s, t: (s, 0, t))
    gate_pre, grad_mixed, stats = pl.pallas_call(
        gate_kernel,
        grid=(seqs, wide_blocks),
        in_specs=[
            by_rows(model),
            by_rows(model),
            fixed((model, 2 * inner), 2),
            by_rows(inner),
            fixed((8, inner), 2),
        ],
        out_specs=[by_rows(inner), by_rows(inner), stats_spec],
        out_shape=[
            seen((seqs, length, inner), BF),
            seen((seqs, length, inner), BF),
            seen((seqs, 8, length)),
        ],
        compiler_params=params(2),
        cost_estimate=cost(27 * 10**9, tokens_here * (4 * model + 8 * inner)),
        name="gate",
    )(normed, cotangent, second_weight, mixed_y, gain_row)

    sums = tensor_sum(stats[:, :2])
    inverse = lax.rsqrt(sums[:, 0] / whole_inner + norm_eps)
    slope = inverse**3 * (sums[:, 1] / whole_inner)
    scales = jnp.pad(jnp.stack([inverse, slope], axis=1), ((0, 0), (0, 6), (0, 0)))

    columns = tensor // 2
    partial_spec = pl.BlockSpec((columns, 1, WIDE_ROWS, share), lambda s, t: (0, s, t, 0))
    scalar_spec = pl.BlockSpec(memory_space=pltpu.SMEM)
    blended, grad_y, grad_gate, out_own, out_other, gain_fold = pl.pallas_call(
        mix_kernel,
        grid=(seqs, wide_blocks),
        in_specs=[
            scalar_spec,
            by_rows(inner),
            by_rows(inner),
            by_rows(inner),
            stats_spec,
            fixed((8, inner), 2),
            pl.BlockSpec((model, inner), lambda s, t: (0, 1)),
        ],
        out_specs=[
            by_rows(inner),
            by_rows(inner),
            by_rows(inner),
            partial_spec,
            partial_spec,
            fixed((8, inner), 2),
        ],
        out_shape=[
            seen((seqs, length, inner), BF),
            seen((seqs, length, inner), BF),
            seen((seqs, length, inner), BF),
            seen((columns, seqs, length, share), BF),
            seen((columns, seqs, length, share), BF),
            seen((8, inner)),
        ],
        compiler_params=params(2),
        cost_estimate=cost(
            28 * 10**9, tokens_here * (2 * model + 14 * inner)
        ),
        name="mix",
    )(starts, mixed_y, gate_pre, grad_mixed, scales, gain_row, second_weight)

    inputs_share = lax.dynamic_slice_in_dim(tokens, share_start, share, 2).astype(F32)

    def weight_grad(left, right):
        return jnp.einsum("std,stu->du", left, right, preferred_element_type=F32)

    out_grad = weight_grad(cotangent, blended).astype(BF)
    grad_gate, out_grad = tie(grad_gate, out_grad)
    gate_grad = weight_grad(normed, grad_gate).astype(BF)
    early_grad = jnp.concatenate([gate_grad, out_grad], axis=1)
    grad_y, early_grad = tie(grad_y, early_grad)
    early_share = lax.psum_scatter(early_grad, "dp", scatter_dimension=0, tiled=True)

    def back(seq, upstream, old):
        def rows_of(width, rows=ROWS):
            return pl.BlockSpec((1, rows, width), lambda i: (seq, blocks - 1 - i, 0))

        per_block = chunks // blocks
        before_spec = pl.BlockSpec(
            (1, 16, inner),
            lambda i: (seq, jnp.maximum((blocks - 1 - i) * (ROWS // 16) - 1, 0), 0),
        )
        shapes = [
            seen((seqs, length, inner), BF),
            seen((seqs, length, states), BF),
            seen((seqs, length, LANES), BF),
            seen((8 * kwidth + 16, inner)),
            seen((16, LANES)),
        ]
        if old is None:
            in_place = (grad_y, conv_bc, step)
            sums = (jnp.zeros(shapes[3].shape, F32), jnp.zeros(shapes[4].shape, F32))
            aliases = {}
        else:
            in_place = old[:3]
            sums = old[3:]
            aliases = {14: 3, 15: 4, 16: 0, 17: 1, 18: 2}
        return pl.pallas_call(
            functools.partial(back_kernel, kwidth),
            grid=(blocks,),
            in_specs=[
                rows_of(inner),
                rows_of(states),
                rows_of(LANES),
                rows_of(LANES),
                rows_of(inner),
                rows_of(inner),
                pl.BlockSpec(
                    (1, per_block, states // 2, inner), lambda i: (seq, blocks - 1 - i, 0, 0)
                ),
                rows_of(inner),
                fixed((8, inner), 1),
                fixed((8, LANES), 1),
                fixed((LANES, inner), 1),
                fixed((2 * LANES, inner), 1),
                fixed((8, inner), 1),
                before_spec,
                fixed(shapes[3].shape, 1),
                fixed(shapes[4].shape, 1),
                any_spec,
                any_spec,
                any_spec,
            ],
            out_specs=[
                rows_of(inner),
                rows_of(states),
                rows_of(LANES),
                fixed(shapes[3].shape, 1),
                fixed(shapes[4].shape, 1),
            ],
            out_shape=shapes,
            scratch_shapes=[
                pltpu.VMEM((states // 2, inner), F32),
                pltpu.VMEM((CHUNK + 8, inner), F32),
                pltpu.VMEM((CHUNK + 16, inner), F32),
            ],
            input_output_aliases=aliases,
            compiler_params=params(1),
            cost_estimate=cost(25 * 10**9, length * inner * 16, length * heads * CHUNK),
            name="back",
        )(
            conv_x,
            conv_bc,
            step,
            cum,
            upstream,
            mixed_y,
            old_states,
            conv_in,
            taps[:, :inner],
            head_rows,
            spread1,
            spread2,
            skip_row,
            conv_in,
            *sums,
            *in_place,
        )

    made = back(0, grad_y, None)
    out_own, *made = tie(out_own, *made)
    arrived = lax.ppermute(out_other, "tensor", [(i, i ^ 1) for i in range(tensor)])
    out_kept, out_leaving = zip(
        *(core_sums(out_own[:, seq], arrived[:, seq]) for seq in range(seqs))
    )
    grad_y, *flat_leaving = tie(grad_y, *sum(out_leaving, []))
    each = columns - 1
    out_leaving = [flat_leaving[i * each : (i + 1) * each] for i in range(seqs)]
    made = back(1, grad_y, made)
    arrivals = [column_sends(sent) for sent in out_leaving]
    grad_in, grad_bc_part, grad_delta, tap_fold, head_fold = back(2, grad_y, made)
    grad_in, *flat_arrivals = tie(grad_in, *sum(arrivals, []))
    arrivals = [flat_arrivals[i * each : (i + 1) * each] for i in range(seqs)]

    bc_chip = chip_total(grad_bc_part)
    in_grad = weight_grad(normed, grad_in).astype(BF)

    in_parts = lax.all_to_all(in_grad, "dp", split_axis=0, concat_axis=0, tiled=True)
    grad_delta, in_grad, bc_chip = tie(grad_delta, in_grad, bc_chip)
    bc_moved = column_total_sends(bc_chip)
    normed_own, normed_other = pl.pallas_call(
        join_kernel,
        grid=(seqs, wide_blocks),
        in_specs=[
            scalar_spec,
            by_rows(inner),
            by_rows(inner),
            by_rows(LANES),
            pl.BlockSpec((model, inner), lambda s, t: (0, 0)),
            pl.BlockSpec((model, inner), lambda s, t: (0, 0)),
            pl.BlockSpec((model, LANES), lambda s, t: (0, (inner + states) // LANES)),
        ],
        out_specs=[partial_spec, partial_spec],
        out_shape=[seen((columns, seqs, length, share), BF)] * 2,
        compiler_params=params(2),
        cost_estimate=cost(33 * 10**9, tokens_here * (2 * model + 4 * inner)),
        name="join",
    )(
        starts,
        grad_gate,
        grad_in,
        grad_delta,
        second_weight,
        first_weight,
        first_weight,
    )
    normed_other, bc_moved = tie(normed_other, bc_moved)
    normed_arrived = lax.ppermute(normed_other, "tensor", [(i, i ^ 1) for i in range(tensor)])
    bc_total = finish_total(bc_chip, bc_moved)
    out_sums = []
    for kept, moved in zip(out_kept, arrivals):
        for part in moved:
            kept = kept + part.astype(F32)
        out_sums.append(kept)
    result = (inputs_share + jnp.stack(out_sums)).astype(BF)

    grad_small, bc_tap_fold = pl.pallas_call(
        functools.partial(bc_kernel, kwidth),
        grid=(seqs,),
        in_specs=[per_seq(states), per_seq(states), fixed((8, states), 1), per_seq(LANES)],
        out_specs=[per_seq(states + LANES), fixed((8 * kwidth + 8, states), 1)],
        out_shape=[
            seen((seqs, length, states + LANES), BF),
            seen((8 * kwidth + 8, states)),
        ],
        scratch_shapes=[
            pltpu.VMEM((length + 8, states), F32),
            pltpu.VMEM((length + 8, states), F32),
        ],
        compiler_params=params(1),
        cost_estimate=cost(8 * 10**9, tokens_here * states * 12),
        name="bc_back",
    )(bc_total, bc_pre, taps[:, inner:], grad_delta)
    small_grad = weight_grad(normed, grad_small).astype(BF)
    small_parts = lax.all_to_all(small_grad, "dp", split_axis=0, concat_axis=0, tiled=True)
    small_grad, normed_own = tie(small_grad, normed_own)
    normed_kept, normed_leaving = core_sums(normed_own, normed_arrived)
    normed_moved = column_sends(normed_leaving)
    early_wide = early_share.astype(F32)
    gate_share = early_wide[:, :inner]
    out_share = early_wide[:, inner:]
    in_share = sum_parts(in_parts)
    small_share = sum_parts(small_parts)
    bc_share = small_share[:, :states]
    dt_share = small_share[:, states : states + heads]
    gate_m = momentum_rate * zx_moment[:, 0, :] + gate_share
    out_m = momentum_rate * out_moment.T + out_share
    in_m = momentum_rate * zx_moment[:, 1, :] + in_share
    bc_m = momentum_rate * bc_moment + bc_share
    dt_m = momentum_rate * dt_moment + dt_share
    early = jnp.concatenate(
        [gate_share + momentum_rate * gate_m, out_share + momentum_rate * out_m], axis=1
    )
    late = jnp.concatenate(
        [in_share + momentum_rate * in_m, bc_share + momentum_rate * bc_m], axis=1
    )
    dt_input = dt_share + momentum_rate * dt_m
    squares = jnp.sum(dt_input * dt_input, axis=0)
    units, slots = gram_units(early, late, squares)
    units, *normed_moved = tie(units, *normed_moved)
    ortho, dt_scale = orthogonal(early, late, units, slots, heads)
    bc_rows = lax.dynamic_slice(first_weight, (share_start, inner), (share, states))
    normed_share = normed_kept
    for moved in normed_moved:
        normed_share = normed_share + moved.astype(F32)
    normed_share = normed_share + jnp.einsum(
        "btk,fk->btf", grad_small[:, :, :states], bc_rows, preferred_element_type=F32
    )

    gain_share = lax.dynamic_slice_in_dim(norm_gain, share_start, share, 0)
    weighted = normed_share * gain_share
    gain_grad_share = jnp.sum(normed_share * inputs_share * inv_rms, axis=(0, 1))
    gain_padded = lax.dynamic_update_slice_in_dim(
        jnp.zeros((model,), F32), gain_grad_share, share_start, 0
    )
    inner_rows = jnp.sum(weighted * inputs_share, axis=-1)
    final_sums = tensor_sum(jnp.concatenate([inner_rows.reshape(-1), gain_padded]))
    inner_sum = final_sums[: seqs * length].reshape(seqs, length)
    gain_part = final_sums[seqs * length :]
    upstream_share = lax.dynamic_slice_in_dim(cotangent, share_start, share, 2).astype(F32)
    input_grad = (
        upstream_share
        + inv_rms * weighted
        - inputs_share * inv_rms**3 * (inner_sum / model)[..., None]
    )

    tap_sums = tap_fold.reshape(kwidth + 2, 8, inner).sum(axis=1)
    head_sums = head_fold.reshape(2, 8, LANES).sum(axis=1)[:, :heads]
    skip_grad = tap_sums[kwidth + 1].reshape(heads, head_width).sum(axis=1)
    pieces = [
        tap_sums[: kwidth + 1].reshape(-1),
        gain_fold.sum(axis=0),
        head_sums.reshape(-1),
        skip_grad,
        bc_tap_fold.reshape(kwidth + 1, 8, states).sum(axis=1).reshape(-1),
        gain_part,
    ]
    flat = dp_sum(jnp.concatenate(pieces))
    xpar_count = (kwidth + 2) * inner
    xpar_g = flat[:xpar_count].reshape(kwidth + 2, inner)
    head_g = flat[xpar_count : xpar_count + 3 * heads].reshape(3, heads)
    bcpar_g = flat[xpar_count + 3 * heads : -model].reshape(kwidth + 1, states)
    gain_g = flat[-model:]

    early_ortho = ortho[:, : 2 * inner]
    late_ortho = ortho[:, 2 * inner :]
    dt_ortho = dt_input * dt_scale
    shrink = 1.0 - matrix_rate * weight_decay
    zx_m = jnp.stack([gate_m, in_m], axis=1)
    zx_new = w_zx * shrink - matrix_rate * jnp.stack(
        [early_ortho[:, :inner], late_ortho[:, :inner]], axis=1
    )
    bc_new = state_proj_weight * shrink - matrix_rate * late_ortho[:, inner:]
    dt_new = step_weight * shrink - matrix_rate * dt_ortho
    out_new = exit_coefficient_matrix * shrink - matrix_rate * early_ortho[:, inner:].T
    gain_m = momentum_rate * gain_moment + gain_g
    xpar_m = momentum_rate * xpar_moment + xpar_g
    bcpar_m = momentum_rate * bcpar_moment + bcpar_g
    head_m = momentum_rate * head_moment + head_g
    gain_new = norm_gain - small_rate * (gain_g + momentum_rate * gain_m)
    xpar_new = x_params - small_rate * (xpar_g + momentum_rate * xpar_m)
    bcpar_new = bc_params - small_rate * (bcpar_g + momentum_rate * bcpar_m)
    head_new = head_params - small_rate * (head_g + momentum_rate * head_m)
    return (
        result,
        input_grad,
        zx_m,
        zx_new,
        bc_m,
        bc_new,
        dt_m,
        dt_new,
        out_m.T,
        out_new,
        gain_m,
        gain_new,
        xpar_m,
        xpar_new,
        bcpar_m,
        bcpar_new,
        head_m,
        head_new,
    )


def solution(mesh):
    return jax.shard_map(
        local,
        mesh=mesh,
        in_specs=(
            P("dp", None, None),
            P("dp", None, None),
            P(),
            P("dp", None, "tensor"),
            P("dp", None),
            P("dp", "tensor"),
            P("tensor", "dp"),
            P(None, "tensor"),
            P(),
            P(None, "tensor"),
            P("dp", None, "tensor"),
            P("dp", None),
            P("dp", "tensor"),
            P("tensor", "dp"),
            P(),
            P(None, "tensor"),
            P(),
            P(None, "tensor"),
        ),
        out_specs=(
            P("dp", None, "tensor"),
            P("dp", None, "tensor"),
            P("dp", None, "tensor"),
            P("dp", None, "tensor"),
            P("dp", None),
            P("dp", None),
            P("dp", "tensor"),
            P("dp", "tensor"),
            P("tensor", "dp"),
            P("tensor", "dp"),
            P(),
            P(),
            P(None, "tensor"),
            P(None, "tensor"),
            P(),
            P(),
            P(None, "tensor"),
            P(None, "tensor"),
        ),
        check_vma=False,
    )
```

time: 1590 us -> 562 us (0.35)
  matrix products: 419 us -> 48.4 us
  local copies, waits for them, and re-layouts: 334 us -> 37.3 us
  blocking collectives: 199 us -> 0 us
  Pallas kernels: 0 us -> 198 us
  waiting for transfers between devices: 329 us -> 131 us
  other arithmetic: 254 us -> 78.1 us
  starting transfers between devices: 9.58 us -> 46.8 us
    dot_general x101 -> x5, matrix products: 419 us -> 48.4 us  [the longest x4 41.8 us: weight_grad(): return jnp.einsum('std,stu->du', left, right, preferred_element_type=F32)]
    reduce_scatter x5 -> x1, waiting for transfers between devices: 322 us -> 0.01 us  [local(): lax.psum_scatter(early_grad, 'dp', scatter_dimension=0, tiled=True)]
    pallas_call x0 -> x12, Pallas kernels: none -> 198 us  [the longest x3 61.2 us: back(): pl.pallas_call(functools.partial(back_kernel, kwidth), grid=(blocks,), in...]
    all_gather x4 -> x0, blocking collectives: 131 us -> none  [the longest x1 36 us: local(): lax.all_gather(state_proj_weight.astype(jnp.bfloat16), 'dp', axis=0, tile...]
    ppermute x0 -> x24, waiting for transfers between devices: none -> 90.8 us  [the longest x4 33.5 us: column_sends(): lax.ppermute(sent, 'tensor', [(i, (i // 2 + shift) % columns * 2 + i % 2)...]
    another operation x47 -> x4, other arithmetic: 94.2 us -> 7.77 us  [the longest x1 5.48 us: local(): result = (inputs_share + jnp.stack(out_sums)).astype(BF)]
    psum x4 -> x0, blocking collectives: 68.1 us -> none  [the longest x1 37.7 us: local(): lax.psum((gain_grad, xpar_local, bcpar_local, grad_head), 'dp')]
    another operation x79 -> x3, local copies, waits for them, and re-layouts: 63.3 us -> 1.52 us  [the longest x1 1.32 us: local(): jnp.stack([early_ortho[:, :inner], late_ortho[:, :inner]], axis=1)]
  transfers between devices with their start and end apart: 11 -> 30, of which waited for: 5 -> 14; matrix products, arithmetic and copies ran while one was open for 36% -> 25% of each run, Pallas kernels for 0% -> 26%
where the time goes in v1:
time: 562 us; the launch traced here: 555 us
  Pallas kernels  198 us (35%)
  waiting for transfers between devices  131 us (23%)
  other arithmetic  78.1 us (14%)
  matrix products  48.4 us (9%)
  starting transfers between devices  46.8 us (8%)
  local copies, waits for them, and re-layouts  37.3 us (7%)
  between operations  15.2 us (3%)
    pallas_call x3, Pallas kernels, back(): pl.pallas_call(functools.partial(back_kernel, kwidth), grid=(blocks,), in...  61.2 us
    dot_general x4, matrix products, weight_grad(): return jnp.einsum('std,stu->du', left, right, preferred_element_type=F32)  41.8 us
    ppermute x4, waiting for transfers between devices, column_sends(): lax.ppermute(sent, 'tensor', [(i, (i // 2 + shift) % columns * 2 + i % 2)...  33.5 us
    pallas_call x1, Pallas kernels, local(): pl.pallas_call(join_kernel, grid=(seqs, wide_blocks), in_specs=[scalar_sp...  27.4 us
    ppermute x3, waiting for transfers between devices, gather_rows(): lax.ppermute(down, 'dp', [(2 * i + j, 2 * i - 2 + j) for i in range(1, 5...  27.3 us
    all_to_all x1, waiting for transfers between devices, local(): lax.all_to_all(in_grad, 'dp', split_axis=0, concat_axis=0, tiled=True)  25.6 us
    pallas_call x1, Pallas kernels, local(): pl.pallas_call(mix_kernel, grid=(seqs, wide_blocks), in_specs=[scalar_spe...  23.4 us
    pallas_call x1, Pallas kernels, local(): pl.pallas_call(functools.partial(project_kernel, kwidth), grid=(seqs, wid...  23.4 us
  transfers between devices with their start and end apart: 30, of which 14 were waited for; matrix products, arithmetic and copies ran while one was open for 25% of the time, Pallas kernels for 26%

profile of v1, /device:TPU:0, one launch (start us, length us, event | category | flops | bytes accessed | tf_op | source)
XLA Modules:
  0.0 555.0 jit_solution(882754023915332303)
XLA Ops:
  20.5 8.2 %collective-permute-done.3 = bf16[192,1152]{1,0:T(8,128)(2,1)S(1)} collective-permute-done((bf16[192,1152]{1,0:T(8,128)(2,1)S(1)}, bf16[192,1152]{1,0:T(8,128)(2,1)S(1)}, u32[]{:S(2)}, u32[]{:S(2)}) %collective-permute-start.3) | collective-permute-done | bytes 442400 | tf_op jit(solution)/shard_map/ppermute | solution.py:716
  31.5 10.5 %collective-permute-done.4 = bf16[192,1152]{1,0:T(8,128)(2,1)S(1)} collective-permute-done((bf16[192,1152]{1,0:T(8,128)(2,1)S(1)}, bf16[192,1152]{1,0:T(8,128)(2,1)S(1)}, u32[]{:S(2)}, u32[]{:S(2)}) %collective-permute-start.4) | collective-permute-done | bytes 442400 | tf_op jit(solution)/shard_map/ppermute | solution.py:716
  45.6 8.7 %collective-permute-done.5 = bf16[192,1152]{1,0:T(8,128)(2,1)S(1)} collective-permute-done((bf16[192,1152]{1,0:T(8,128)(2,1)S(1)}, bf16[192,1152]{1,0:T(8,128)(2,1)S(1)}, u32[]{:S(2)}, u32[]{:S(2)}) %collective-permute-start.5) | collective-permute-done | bytes 442400 | tf_op jit(solution)/shard_map/ppermute | solution.py:716
  73.3 9.5 %fusion.2.normed = bf16[3,1024,1536]{2,1,0:T(8,128)(2,1)} fusion(bf16[3,1024,1536]{2,1,0:T(8,128)(2,1)} %param.18, f32[1536]{0:T(1024)S(1)} %copy-done.18, f32[3,1024]{1,0:T(4,128)S(1)} %get-tuple-element.245), kind=kLoop, calls=%fused_computation.4 | loop fusion | flops 18874368 | bytes 18892800 | tf_op jit(solution)/shard_map/convert_element_type | solution.py:878
  82.8 21.6 %collective-permute-done.7 = bf16[576,1152]{1,0:T(8,128)(2,1)S(1)} collective-permute-done((bf16[576,1152]{1,0:T(8,128)(2,1)S(1)}, bf16[576,1152]{1,0:T(8,128)(2,1)S(1)}, u32[]{:S(2)}, u32[]{:S(2)}) %collective-permute-start.7) | collective-permute-done | bytes 1327136 | tf_op jit(solution)/shard_map/ppermute | solution.py:727
  106.8 23.4 %project.1 = (bf16[3,1024,768]{2,1,0:T(8,128)(2,1)}, f32[3,1024,256]{2,1,0:T(8,128)}, bf16[3,1024,768]{2,1,0:T(8,128)(2,1)}, bf16[3,1024,256]{2,1,0:T(8,128)(2,1...) custom-call(bf16[3,1024,1536]{2,1,0:T(8,128)(2,1)} %fusion.2.normed, ...), custom_call_target="tpu_custom_call" | custom-call | flops 700000000 | bytes 589824 | tf_op jit(solution)/shard_map/project/pallas_call | solution.py:892
  130.2 18.1 %scan.1 = (f32[3,1024,768]{2,1,0:T(8,128)}, bf16[3,8,128,768]{3,2,1,0:T(8,128)(2,1)}) custom-call(bf16[3,1024,768]{2,1,0:T(8,128)(2,1)} %get-tuple-element.82.conv_x, bf16[3,1024,256]{2,1,0:T(8,128)(2,1)S(1)} %get-tuple-element.83.conv_bc.after_bc, f32[3,1024,128]{2,1,0:T(8,128)} %get-tuple-element.84.step.after_delta, ...), custom_call_target="tpu_custom_call" | custom-call | flops 500000000 | bytes 471859 | tf_op jit(solution)/shard_map/scan/pallas_call | solution.py:929
  148.3 23.2 %gate.1 = (bf16[3,1024,768]{2,1,0:T(8,128)(2,1)}, bf16[3,1024,768]{2,1,0:T(8,128)(2,1)}, f32[3,8,1024]{2,1,0:T(8,128)S(1)}) custom-call(bf16[3,1024,1536]{2,1,0:T(8,128)(2,1)} %fusion.2.normed, bf16[3,1024,1536]{2,1,0:T(8,128)(2,1)} %cotangent.1, bf16[1536,1536]{1,0:T(8,128)(2,1)} %all-gather.2.cloned.1.call-done.weight.gate_weight, ...), custom_call_target="tpu_custom_call" | custom-call | flops 675000000 | bytes 943718 | tf_op jit(solution)/shard_map/gate/pallas_call | solution.py:954
  176.8 23.4 %mix.1 = (bf16[3,1024,768]{2,1,0:T(8,128)(2,1)}, bf16[3,1024,768]{2,1,0:T(8,128)(2,1)}, bf16[3,1024,768]{2,1,0:T(8,128)(2,1)}, bf16[2,3,1024,384]{3,2,1,0:T(8,12...) custom-call(s32[4]{0:T(128)S(1)} %add_multiply_fusion.starts, f32[3,1024,768]{2,1,0:T(8,128)} %get-tuple-element.86.y, ...), custom_call_target="tpu_custom_call" | custom-call | flops 700000000 | bytes 1061683 | tf_op jit(solution)/shard_map/mix/pallas_call | solution.py:983
  200.2 12.0 %fusion.10 = bf16[1536,768]{1,0:T(8,128)(2,1)S(1)} fusion(bf16[3,1024,768]{2,1,0:T(8,128)(2,1)} %get-tuple-element.94, bf16[3,1024,1536]{2,1,0:T(8,128)(2,1)} %cotangent.1), kind=kOutput, calls=%fused_computation.23 | convolution fusion | flops 7248936960 | bytes 16515072 | tf_op jit(solution)/shard_map/std,stu->du/dot_general | solution.py:1021
  212.3 7.9 %bitcast_convert_fusion.1 = bf16[1536,768]{1,0:T(8,128)(2,1)S(1)} fusion(bf16[3,1024,1536]{2,1,0:T(8,128)(2,1)S(1)} %bitcast.122, bf16[3,1024,768]{2,1,0:T(8,128)(2,1)S(1)} %copy-done.4), kind=kOutput, calls=%fused_computation.19 | convolution fusion | flops 7248936960 | bytes 16515072 | tf_op jit(solution)/shard_map/std,stu->du/dot_general | solution.py:1021
  222.7 20.6 %back.3 = (bf16[3,1024,768]{2,1,0:T(8,128)(2,1)}, bf16[3,1024,256]{2,1,0:T(8,128)(2,1)}, bf16[3,1024,128]{2,1,0:T(8,128)(2,1)S(1)}, f32[48,768]{1,0:T(8,128)S(1)}, f32[16,128]{1,0:T(8,128)S(1)}) custom-call(bf16[3,1024,768]{2,1,0:T(8,128)(2,1)} %get-tuple-element.82.conv_x, bf16[3,1024,256]{2,1,0:T(8,128)(2,1)} %copy-done, ...), custom_call_target="tpu_custom_call" | custom-call | flops 625000000 | bytes 314572 | tf_op jit(solution)/shard_map/back/pallas_call | solution.py:1054
  249.6 20.2 %back.4 = (bf16[3,1024,768]{2,1,0:T(8,128)(2,1)}, bf16[3,1024,256]{2,1,0:T(8,128)(2,1)}, bf16[3,1024,128]{2,1,0:T(8,128)(2,1)S(1)}, f32[48,768]{1,0:T(8,128)S(1)}, f32[16,128]{1,0:T(8,128)S(1)}) custom-call(bf16[3,1024,768]{2,1,0:T(8,128)(2,1)} %get-tuple-element.82.conv_x, ...), custom_call_target="tpu_custom_call", output_to_operand_aliasing={{3}: (14, {}), {4}: (15, {}), {0}: (16, {}), {1}: (17, {}),... | custom-call | flops 625000000 | bytes 314572 | tf_op jit(solution)/shard_map/back/pallas_call | solution.py:1054
  269.8 20.4 %back.5 = (bf16[3,1024,768]{2,1,0:T(8,128)(2,1)}, bf16[3,1024,256]{2,1,0:T(8,128)(2,1)}, bf16[3,1024,128]{2,1,0:T(8,128)(2,1)S(1)}, f32[48,768]{1,0:T(8,128)S(1)}, f32[16,128]{1,0:T(8,128)S(1)}) custom-call(bf16[3,1024,768]{2,1,0:T(8,128)(2,1)} %get-tuple-element.82.conv_x, ...), custom_call_target="tpu_custom_call", output_to_operand_aliasing={{3}: (14, {}), {4}: (15, {}), {0}: (16, {}), {1}: (17, {}),... | custom-call | flops 625000000 | bytes 314572 | tf_op jit(solution)/shard_map/back/pallas_call | solution.py:1054
  290.3 11.1 %collective-permute-done.13 = bf16[1024,384]{1,0:T(8,128)(2,1)} collective-permute-done((bf16[1024,384]{1,0:T(8,128)(2,1)}, bf16[1024,384]{1,0:T(8,128)(2,1)}, u32[]{:S(2)}, u32[]{:S(2)}) %collective-permute-start.13) | collective-permute-done | bytes 786464 | tf_op jit(solution)/shard_map/ppermute | solution.py:661
  301.4 12.7 %bitcast_convert_fusion = bf16[1536,768]{1,0:T(8,128)(2,1)} fusion(bf16[3,1024,1536]{2,1,0:T(8,128)(2,1)} %fusion.2.normed, bf16[3,1024,768]{2,1,0:T(8,128)(2,1)} %get-tuple-element.126.grad_in), kind=kOutput, calls=%fused_computation.18 | convolution fusion | flops 7248936960 | bytes 16515072 | tf_op jit(solution)/shard_map/std,stu->du/dot_general | solution.py:1021
  314.7 27.4 %join.1 = (bf16[2,3,1024,384]{3,2,1,0:T(8,128)(2,1)}, bf16[2,3,1024,384]{3,2,1,0:T(8,128)(2,1)}) custom-call(s32[4]{0:T(128)S(1)} %add_multiply_fusion.starts, bf16[3,1024,768]{2,1,0:T(8,128)(2,1)} %get-tuple-element.95.grad_gate, bf16[3,1024,768]{2,1,0:T(8,128)(2,1)} %get-tuple-element.126.grad_in, bf16[3,1024,128]{2,1,0:T(8,128)(2,1)S(1)} %get-tuple-element.129.grad_delta, ...), custom_call_target="tpu_custom_call" | custom-call | flops 825000000 | bytes 471859 | tf_op jit(solution)/shard_map/join/pallas_call | solution.py:1137
  343.0 9.2 %all-to-all-start = ((bf16[8,192,768]{2,1,0:T(8,128)(2,1)}), bf16[8,192,768]{2,1,0:T(8,128)(2,1)}, u32[]{:S(2)}, u32[]{:S(2)}) async-start(bf16[8,192,768]{2,1,0:T(8,128)(2,1)} %bitcast.123), calls=%async_computation.1 | async-start | bytes 4718592 | tf_op jit(solution)/shard_map/all_to_all | solution.py:1134
  363.3 8.7 %bc_back.1 = (bf16[3,1024,384]{2,1,0:T(8,128)(2,1)}, f32[40,256]{1,0:T(8,128)S(1)}) custom-call(bf16[3,1024,256]{2,1,0:T(8,128)(2,1)} %pad_maximum_fusion.1.summed, f32[3,1024,256]{2,1,0:T(8,128)} %get-tuple-element.132.pre, f32[8,256]{1,0:T(8,128)S(1)} %slice.254.taps, bf16[3,1024,128]{2,1,0:T(8,128)(2,1)S(1)} %get-tuple-element.129.grad_delta), custom_call_target="tpu_custom_call" | custom-call | flops 200000000 | bytes 235929 | tf_op jit(solution)/shard_map/bc_back/pallas_call | solution.py:1173
  372.0 9.2 %fusion.11 = bf16[1536,384]{1,0:T(8,128)(2,1)} fusion(bf16[3,1024,1536]{2,1,0:T(8,128)(2,1)} %fusion.2.normed, bf16[3,1024,384]{2,1,0:T(8,128)(2,1)} %get-tuple-element.133), kind=kOutput, calls=%fused_computation.25 | convolution fusion | flops 3624468480 | bytes 12976128 | tf_op jit(solution)/shard_map/std,stu->du/dot_general | solution.py:1021
  381.2 25.6 %all-to-all-done = bf16[8,192,768]{2,1,0:T(8,128)(2,1)} async-done(((bf16[8,192,768]{2,1,0:T(8,128)(2,1)}), bf16[8,192,768]{2,1,0:T(8,128)(2,1)}, u32[]{:S(2)}, u32[]{:S(2)}) %all-to-all-start) | async-done | bytes 2359328 | tf_op jit(solution)/shard_map/all_to_all | solution.py:1134
  431.0 8.4 %all-to-all-done.1 = bf16[8,192,384]{2,1,0:T(8,128)(2,1)} async-done(((bf16[8,192,384]{2,1,0:T(8,128)(2,1)}), bf16[8,192,384]{2,1,0:T(8,128)(2,1)}, u32[]{:S(2)}, u32[]{:S(2)}) %all-to-all-start.1) | async-done | bytes 1179680 | tf_op jit(solution)/shard_map/all_to_all | solution.py:1191
  446.5 22.3 %collective-permute-done.18 = bf16[3,1024,384]{2,1,0:T(8,128)(2,1)} collective-permute-done((bf16[3,1024,384]{2,1,0:T(8,128)(2,1)}, bf16[3,1024,384]{2,1,0:T(8,128)(2,1)}, u32[]{:S(2)}, u32[]{:S(2)}) %collective-permute-start.18) | collective-permute-done | bytes 2359328 | tf_op jit(solution)/shard_map/ppermute | solution.py:661
  505.6 9.0 %fusion.5 = (f32[3,1024,384]{2,1,0:T(8,128)}, bf16[3,1024,384]{2,1,0:T(8,128)(2,1)}) fusion(f32[3,1024,384]{2,1,0:T(8,128)} %get-tuple-element.246, f32[3,1024]{1,0:T(4,128)} %div.65, f32[3,1024]{1,0:T(4,128)} %get-tuple-element.244, f32[384]{0:T(512)} %dynamic_slice.35, f32[3,1024]{1,0:T(4,128)S(1)} %get-tuple-element.245, ...), kind=kLoop, calls=%fused_computation.11 | loop fusion | flops 14155776 | bytes 21272068 | tf_op jit(solution)/shard_map/sub | solution.py:1238
  (228 shorter events, 168.6 us)
Async XLA Ops:
  7.2 141.1 %all-gather.2.cloned.1.call-start = ((), (), s32[]{:S(2)}) async-start(), calls=%async_computation.5 | async-start | bytes 5308416 | tf_op jit(solution)/shard_map/all_gather | solution.py:873
  13.7 15.1 %collective-permute-start.3 = (bf16[192,1152]{1,0:T(8,128)(2,1)S(1)}, bf16[192,1152]{1,0:T(8,128)(2,1)S(1)}, u32[]{:S(2)}, u32[]{:S(2)}) collective-permute-start(bf16[192,1152]{1,0:T(8,128)(2,1)S(1)} %get-tuple-element.241), channel_id=1, source_target_pairs={{8,0},{12,4},{16,8},{20,12},{24,16},{28,20},{9,1},{13,5},{17,9},{2... | collective-permute-start | bytes 1327112 | tf_op jit(solution)/shard_map/ppermute | solution.py:716
  15.0 15.1 %collective-permute-start = (bf16[192,1152]{1,0:T(8,128)(2,1)S(1)}, bf16[192,1152]{1,0:T(8,128)(2,1)S(1)}, u32[]{:S(2)}, u32[]{:S(2)}) collective-permute-start(bf16[192,1152]{1,0:T(8,128)(2,1)S(1)} %get-tuple-element.241), channel_id=1, source_target_pairs={{0,8},{4,12},{8,16},{12,20},{16,24},{20,28},{1,9},{5,13},{9,17},{1... | collective-permute-start | bytes 1327112 | tf_op jit(solution)/shard_map/ppermute | solution.py:713
  28.7 13.2 %collective-permute-start.4 = (bf16[192,1152]{1,0:T(8,128)(2,1)S(1)}, bf16[192,1152]{1,0:T(8,128)(2,1)S(1)}, u32[]{:S(2)}, u32[]{:S(2)}) collective-permute-start(bf16[192,1152]{1,0:T(8,128)(2,1)S(1)} %collective-permute-done.3), channel_id=1, source_target_pairs={{8,0},{12,4},{16,8},{20,12},{9,1},{13,5},{17,9},{21,13},{10,2},{14... | collective-permute-start | bytes 1327112 | tf_op jit(solution)/shard_map/ppermute | solution.py:716
  30.0 13.2 %collective-permute-start.1 = (bf16[192,1152]{1,0:T(8,128)(2,1)S(1)}, bf16[192,1152]{1,0:T(8,128)(2,1)}, u32[]{:S(2)}, u32[]{:S(2)}) collective-permute-start(bf16[192,1152]{1,0:T(8,128)(2,1)S(1)} %collective-permute-done), channel_id=1, source_target_pairs={{8,16},{12,20},{16,24},{20,28},{9,17},{13,21},{17,25},{21,29},{10,... | collective-permute-start | bytes 1327112 | tf_op jit(solution)/shard_map/ppermute | solution.py:713
  42.0 12.3 %collective-permute-start.5 = (bf16[192,1152]{1,0:T(8,128)(2,1)S(1)}, bf16[192,1152]{1,0:T(8,128)(2,1)S(1)}, u32[]{:S(2)}, u32[]{:S(2)}) collective-permute-start(bf16[192,1152]{1,0:T(8,128)(2,1)S(1)} %collective-permute-done.4), channel_id=1, source_target_pairs={{8,0},{12,4},{9,1},{13,5},{10,2},{14,6},{11,3},{15,7}} | collective-permute-start | bytes 1327112 | tf_op jit(solution)/shard_map/ppermute | solution.py:716
  43.3 11.0 %collective-permute-start.2 = (bf16[192,1152]{1,0:T(8,128)(2,1)}, bf16[192,1152]{1,0:T(8,128)(2,1)}, u32[]{:S(2)}, u32[]{:S(2)}) collective-permute-start(bf16[192,1152]{1,0:T(8,128)(2,1)} %collective-permute-done.1), channel_id=1, source_target_pairs={{16,24},{20,28},{17,25},{21,29},{18,26},{22,30},{19,27},{23,31}} | collective-permute-start | bytes 1327112 | tf_op jit(solution)/shard_map/ppermute | solution.py:713
  54.3 369.1 %reduce-scatter.2.cloned.1.call-start = ((), (), s32[]{:S(2)}) async-start(), calls=%async_computation.6 | async-start | bytes 5308416 | tf_op jit(solution)/shard_map/reduce_scatter | solution.py:1028
  54.4 9.6 %collective-permute-start.6 = (bf16[192,1152]{1,0:T(8,128)(2,1)S(1)}, bf16[192,1152]{1,0:T(8,128)(2,1)S(1)}, u32[]{:S(2)}, u32[]{:S(2)}) collective-permute-start(bf16[192,1152]{1,0:T(8,128)(2,1)S(1)} %get-tuple-element.241), channel_id=1, source_target_pairs={{0,4},{4,0},{8,12},{12,8},{16,20},{20,16},{24,28},{28,24},{1,5},{5... | collective-permute-start | bytes 1327112 | tf_op jit(solution)/shard_map/ppermute | solution.py:709
  66.4 38.1 %collective-permute-start.7 = (bf16[576,1152]{1,0:T(8,128)(2,1)S(1)}, bf16[576,1152]{1,0:T(8,128)(2,1)S(1)}, u32[]{:S(2)}, u32[]{:S(2)}) collective-permute-start(bf16[576,1152]{1,0:T(8,128)(2,1)S(1)} %pad_maximum_fusion.2), channel_id=1, source_target_pairs={{0,4},{4,0},{8,12},{12,8},{16,20},{20,16},{24,28},{28,24},{1,5},{5... | collective-permute-start | bytes 3981320 | tf_op jit(solution)/shard_map/ppermute | solution.py:727
  200.2 43.2 %collective-permute-start.10 = (bf16[2,3,1024,384]{3,2,1,0:T(8,128)(2,1)}, bf16[2,3,1024,384]{3,2,1,0:T(8,128)(2,1)}, u32[]{:S(2)}, u32[]{:S(2)}) collective-permute-start(bf16[2,3,1024,384]{3,2,1,0:T(8,128)(2,1)} %get-tuple-element.106), channel_id=1, source_target_pairs={{0,1},{1,0},{2,3},{3,2},{4,5},{5,4},{6,7},{7,6},{8,9},{9,8},{10,11... | collective-permute-start | bytes 14155784 | tf_op jit(solution)/shard_map/ppermute | solution.py:1118
  247.5 42.7 %collective-permute-start.11 = (bf16[1024,384]{1,0:T(8,128)(2,1)}, bf16[1024,384]{1,0:T(8,128)(2,1)S(1)}, u32[]{:S(2)}, u32[]{:S(2)}) collective-permute-start(bf16[1024,384]{1,0:T(8,128)(2,1)} %get-tuple-element.119), channel_id=1, source_target_pairs={{0,2},{1,3},{2,0},{3,1},{4,6},{5,7},{6,4},{7,5},{8,10},{9,11},{10,... | collective-permute-start | bytes 2359304 | tf_op jit(solution)/shard_map/ppermute | solution.py:661
  247.5 42.8 %collective-permute-start.12 = (bf16[1024,384]{1,0:T(8,128)(2,1)}, bf16[1024,384]{1,0:T(8,128)(2,1)S(1)}, u32[]{:S(2)}, u32[]{:S(2)}) collective-permute-start(bf16[1024,384]{1,0:T(8,128)(2,1)} %get-tuple-element.120), channel_id=1, source_target_pairs={{0,2},{1,3},{2,0},{3,1},{4,6},{5,7},{6,4},{7,5},{8,10},{9,11},{10,... | collective-permute-start | bytes 2359304 | tf_op jit(solution)/shard_map/ppermute | solution.py:661
  249.5 51.9 %collective-permute-start.13 = (bf16[1024,384]{1,0:T(8,128)(2,1)}, bf16[1024,384]{1,0:T(8,128)(2,1)}, u32[]{:S(2)}, u32[]{:S(2)}) collective-permute-start(bf16[1024,384]{1,0:T(8,128)(2,1)} %get-tuple-element.121), channel_id=1, source_target_pairs={{0,2},{1,3},{2,0},{3,1},{4,6},{5,7},{6,4},{7,5},{8,10},{9,11},{10,... | collective-permute-start | bytes 2359304 | tf_op jit(solution)/shard_map/ppermute | solution.py:661
  290.2 23.9 %collective-permute-start.14 = (bf16[3,1024,256]{2,1,0:T(8,128)(2,1)}, bf16[3,1024,256]{2,1,0:T(8,128)(2,1)S(1)}, u32[]{:S(2)}, u32[]{:S(2)}) collective-permute-start(bf16[3,1024,256]{2,1,0:T(8,128)(2,1)} %get-tuple-element.127), channel_id=1, source_target_pairs={{0,1},{1,0},{2,3},{3,2},{4,5},{5,4},{6,7},{7,6},{8,9},{9,8},{10,11... | collective-permute-start | bytes 4718600 | tf_op jit(solution)/shard_map/ppermute | solution.py:746
  314.4 27.7 %collective-permute-start.15 = (bf16[3,512,256]{2,1,0:T(8,128)(2,1)S(1)}, bf16[3,512,256]{2,1,0:T(8,128)(2,1)S(1)}, u32[]{:S(2)}, u32[]{:S(2)}) collective-permute-start(bf16[3,512,256]{2,1,0:T(8,128)(2,1)S(1)} %add_convert_fusion.2), channel_id=1, source_target_pairs={{0,2},{1,3},{2,0},{3,1},{4,6},{5,7},{6,4},{7,5},{8,10},{9,11},{10,... | collective-permute-start | bytes 2359304 | tf_op jit(solution)/shard_map/ppermute | solution.py:756
  343.0 68.6 %collective-permute-start.17 = (bf16[2,3,1024,384]{3,2,1,0:T(8,128)(2,1)}, bf16[2,3,1024,384]{3,2,1,0:T(8,128)(2,1)}, u32[]{:S(2)}, u32[]{:S(2)}) collective-permute-start(bf16[2,3,1024,384]{3,2,1,0:T(8,128)(2,1)} %get-tuple-element.136), channel_id=1, source_target_pairs={{0,1},{1,0},{2,3},{3,2},{4,5},{5,4},{6,7},{7,6},{8,9},{9,8},{10,11... | collective-permute-start | bytes 14155784 | tf_op jit(solution)/shard_map/ppermute | solution.py:1164
  343.0 63.8 %all-to-all-start = ((bf16[8,192,768]{2,1,0:T(8,128)(2,1)}), bf16[8,192,768]{2,1,0:T(8,128)(2,1)}, u32[]{:S(2)}, u32[]{:S(2)}) async-start(bf16[8,192,768]{2,1,0:T(8,128)(2,1)} %bitcast.123), calls=%async_computation.1 | async-start | bytes 4718592 | tf_op jit(solution)/shard_map/all_to_all | solution.py:1134
  406.8 32.7 %all-to-all-start.1 = ((bf16[8,192,384]{2,1,0:T(8,128)(2,1)}), bf16[8,192,384]{2,1,0:T(8,128)(2,1)}, u32[]{:S(2)}, u32[]{:S(2)}) async-start(bf16[8,192,384]{2,1,0:T(8,128)(2,1)} %bitcast.23), calls=%async_computation.2 | async-start | bytes 2359296 | tf_op jit(solution)/shard_map/all_to_all | solution.py:1191
  416.0 52.9 %collective-permute-start.18 = (bf16[3,1024,384]{2,1,0:T(8,128)(2,1)}, bf16[3,1024,384]{2,1,0:T(8,128)(2,1)}, u32[]{:S(2)}, u32[]{:S(2)}) collective-permute-start(bf16[3,1024,384]{2,1,0:T(8,128)(2,1)} %fusion.12), channel_id=1, source_target_pairs={{0,2},{1,3},{2,0},{3,1},{4,6},{5,7},{6,4},{7,5},{8,10},{9,11},{10,... | collective-permute-start | bytes 7077896 | tf_op jit(solution)/shard_map/ppermute | solution.py:661
  477.0 37.7 %all-to-all-start.2 = ((f32[24,64,128]{2,1,0:T(8,128)}), f32[24,64,128]{2,1,0:T(8,128)S(1)}, u32[]{:S(2)}, u32[]{:S(2)}) async-start(f32[24,64,128]{2,1,0:T(8,128)} %shard_map.313), calls=%async_computation.3 | async-start | bytes 1572864 | tf_op jit(solution)/shard_map/all_to_all | solution.py:806
  497.5 6.7 %collective-permute-start.22 = (f32[7460]{0:T(1024)}, f32[7460]{0:T(1024)}, u32[]{:S(2)}, u32[]{:S(2)}) collective-permute-start(f32[7460]{0:T(1024)} %add.424), channel_id=1, source_target_pairs={{0,8},{4,12},{8,0},{12,4},{16,24},{20,28},{24,16},{28,20},{1,9},{5... | collective-permute-start | bytes 89528 | tf_op jit(solution)/shard_map/ppermute | solution.py:777
  504.9 9.7 %collective-permute-start.23 = (f32[7460]{0:T(1024)S(1)}, f32[7460]{0:T(1024)S(1)}, u32[]{:S(2)}, u32[]{:S(2)}) collective-permute-start(f32[7460]{0:T(1024)S(1)} %add.425), channel_id=1, source_target_pairs={{0,16},{4,20},{8,24},{12,28},{16,0},{20,4},{24,8},{28,12},{1,17},{... | collective-permute-start | bytes 89528 | tf_op jit(solution)/shard_map/ppermute | solution.py:777
  520.3 14.9 %all-to-all-start.3 = ((bf16[8,3,64,128]{3,2,1,0:T(8,128)(2,1)}), bf16[8,3,64,128]{3,2,1,0:T(8,128)(2,1)S(1)}, u32[]{:S(2)}, u32[]{:S(2)}) async-start(bf16[8,3,64,128]{3,2,1,0:T(8,128)(2,1)} %broadcast_in_dim.57), calls=%async_computation.4 | async-start | bytes 786432 | tf_op jit(solution)/shard_map/all_to_all | solution.py:629
  (33 other events, 588.9 us)
Sparse Core Ops, SparseCore 0:
  54.4 86.2 all-gather.1
  222.8 98.4 reduce-scatter.1

commit v2 on v1

--- a/solution.py
+++ b/solution.py
@@ -165,13 +165,13 @@
         for pair in range(inner // LANES):
             cols = slice(pair * LANES, (pair + 1) * LANES)
             pair_x = value[:, cols]
-            parts = []
+            stacked = []
             for head in (2 * pair, 2 * pair + 1):
                 gap = running[:, head : head + 1] - keys[head : head + 1, :]
-                kernel = jnp.where(causal, jnp.exp(gap) * scores, 0.0).astype(BF)
-                parts.append(dot(kernel, pair_x))
+                stacked.append(jnp.where(causal, jnp.exp(gap) * scores, 0.0).astype(BF))
+            parts = dot(jnp.concatenate(stacked, axis=0), pair_x)
             y[0, rows, cols] = (
-                jnp.where(first, parts[0], parts[1])
+                jnp.where(first, parts[:CHUNK], parts[CHUNK:])
                 + carried[:, cols] * grow[:, cols]
                 + skip[0:1, cols] * pair_x.astype(F32)
             )
@@ -362,18 +362,24 @@
             cols = slice(pair * LANES, (pair + 1) * LANES)
             pair_x = value[:, cols]
             pair_up = upstream[:, cols]
-            parts = []
-            for side in (0, 1):
-                head = 2 * pair + side
+            kernels = []
+            for head in (2 * pair, 2 * pair + 1):
                 gap = queries[head : head + 1, :] - keys[:, head : head + 1]
-                kernel = jnp.where(anti, jnp.exp(gap), 0.0)
-                own_x = jnp.where(first if side == 0 else ~first, pair_x, jnp.zeros_like(pair_x))
-                score_grad = score_grad + kernel * dot_nt(own_x, pair_up)
-                parts.append(dot((kernel * scores).astype(BF), pair_up))
+                kernels.append(jnp.where(anti, jnp.exp(gap), 0.0))
+            nothing = jnp.zeros_like(pair_x)
+            own_x = jnp.concatenate(
+                [jnp.where(first, pair_x, nothing), jnp.where(first, nothing, pair_x)], axis=0
+            )
+            products = dot_nt(own_x, pair_up)
+            score_grad = (
+                score_grad + kernels[0] * products[:CHUNK] + kernels[1] * products[CHUNK:]
+            )
+            stacked = [(kernel * scores).astype(BF) for kernel in kernels]
+            parts = dot(jnp.concatenate(stacked, axis=0), pair_up)
             x_wide = pair_x.astype(F32)
             up_wide = pair_up.astype(F32)
             far = reach[:, cols] * tail[:, cols]
-            inside = jnp.where(first, parts[0], parts[1]) + far
+            inside = jnp.where(first, parts[:CHUNK], parts[CHUNK:]) + far
             skip_row = skip[0:1, cols]
             pull = x_wide * inside
             pull_parts.append(pull)
@@ -716,6 +722,8 @@
         down = lax.ppermute(
             down, "dp", [(2 * i + j, 2 * i - 2 + j) for i in range(1, 5 - step) for j in range(2)]
         )
+        if step == 1:
+            up, down, other = tie(up, down, other)
         result = place(place(result, up, z - step, y), down, z + step, y)
     leaving = jnp.concatenate(
         [
@@ -798,7 +806,7 @@
     return units, slots
 
 
-def orthogonal(first, second, units, slots, count):
+def newton(units, slots):
     dp = lax.axis_size("dp")
     half = LANES // 2
     each = units.shape[0] // dp
@@ -817,6 +825,14 @@
     factors = whole_call(
         newton_kernel, seen((each, half, LANES), BF), parts.reshape(dp, each, half, LANES), kinds
     )
+    return factors
+
+
+def updates(first, second, factors, slots, count):
+    dp = lax.axis_size("dp")
+    half = LANES // 2
+    each = factors.shape[0]
+    single = slots[2]
     factors = copy_to_all(factors, "dp").reshape(dp * each, half, LANES)
     made = whole_call(
         functools.partial(apply_kernel, slots),
@@ -1113,15 +1129,15 @@
             *in_place,
         )
 
-    made = back(0, grad_y, None)
-    out_own, *made = tie(out_own, *made)
     arrived = lax.ppermute(out_other, "tensor", [(i, i ^ 1) for i in range(tensor)])
+    grad_y, out_own, arrived = tie(grad_y, out_own, arrived)
     out_kept, out_leaving = zip(
         *(core_sums(out_own[:, seq], arrived[:, seq]) for seq in range(seqs))
     )
     grad_y, *flat_leaving = tie(grad_y, *sum(out_leaving, []))
     each = columns - 1
     out_leaving = [flat_leaving[i * each : (i + 1) * each] for i in range(seqs)]
+    made = back(0, grad_y, None)
     made = back(1, grad_y, made)
     arrivals = [column_sends(sent) for sent in out_leaving]
     grad_in, grad_bc_part, grad_delta, tap_fold, head_fold = back(2, grad_y, made)
@@ -1160,9 +1176,14 @@
         first_weight,
         first_weight,
     )
-    normed_other, bc_moved = tie(normed_other, bc_moved)
+    normed_own, normed_other, bc_moved, in_parts = tie(
+        normed_own, normed_other, bc_moved, in_parts
+    )
     normed_arrived = lax.ppermute(normed_other, "tensor", [(i, i ^ 1) for i in range(tensor)])
+    normed_kept, normed_leaving = core_sums(normed_own, normed_arrived)
     bc_total = finish_total(bc_chip, bc_moved)
+    bc_total, *normed_leaving = tie(bc_total, *normed_leaving)
+    normed_moved = column_sends(normed_leaving)
     out_sums = []
     for kept, moved in zip(out_kept, arrivals):
         for part in moved:
@@ -1189,9 +1210,6 @@
     )(bc_total, bc_pre, taps[:, inner:], grad_delta)
     small_grad = weight_grad(normed, grad_small).astype(BF)
     small_parts = lax.all_to_all(small_grad, "dp", split_axis=0, concat_axis=0, tiled=True)
-    small_grad, normed_own = tie(small_grad, normed_own)
-    normed_kept, normed_leaving = core_sums(normed_own, normed_arrived)
-    normed_moved = column_sends(normed_leaving)
     early_wide = early_share.astype(F32)
     gate_share = early_wide[:, :inner]
     out_share = early_wide[:, inner:]
@@ -1213,8 +1231,7 @@
     dt_input = dt_share + momentum_rate * dt_m
     squares = jnp.sum(dt_input * dt_input, axis=0)
     units, slots = gram_units(early, late, squares)
-    units, *normed_moved = tie(units, *normed_moved)
-    ortho, dt_scale = orthogonal(early, late, units, slots, heads)
+    factors = newton(units, slots)
     bc_rows = lax.dynamic_slice(first_weight, (share_start, inner), (share, states))
     normed_share = normed_kept
     for moved in normed_moved:
@@ -1231,6 +1248,7 @@
     )
     inner_rows = jnp.sum(weighted * inputs_share, axis=-1)
     final_sums = tensor_sum(jnp.concatenate([inner_rows.reshape(-1), gain_padded]))
+    final_sums, factors = tie(final_sums, factors)
     inner_sum = final_sums[: seqs * length].reshape(seqs, length)
     gain_part = final_sums[seqs * length :]
     upstream_share = lax.dynamic_slice_in_dim(cotangent, share_start, share, 2).astype(F32)
@@ -1258,6 +1276,7 @@
     bcpar_g = flat[xpar_count + 3 * heads : -model].reshape(kwidth + 1, states)
     gain_g = flat[-model:]
 
+    ortho, dt_scale = updates(early, late, factors, slots, heads)
     early_ortho = ortho[:, : 2 * inner]
     late_ortho = ortho[:, 2 * inner :]
     dt_ortho = dt_input * dt_scale

time: 562 us -> 571 us (1.016)
  waiting for transfers between devices: 131 us -> 158 us
  local copies, waits for them, and re-layouts: 37.3 us -> 29.2 us
  other arithmetic: 78.1 us -> 72.1 us
    all_to_all x1, waiting for transfers between devices: 25.6 us -> 58.6 us  [local(): lax.all_to_all(in_grad, 'dp', split_axis=0, concat_axis=0, tiled=True)]
    ppermute x4, waiting for transfers between devices: 33.5 us -> 10.6 us  [column_sends(): lax.ppermute(sent, 'tensor', [(i, (i // 2 + shift) % columns * 2 + i % 2)...]
    ppermute x1, waiting for transfers between devices: 0.01 us -> 6.15 us  [finish_total(): other = lax.ppermute(part, 'tensor', [(i, i ^ 1) for i in range(count)])]
    all_to_all x1, waiting for transfers between devices: 5.95 us -> 0.01 us  [copy_to_all(): lax.all_to_all(jnp.broadcast_to(array, (count,) + array.shape), axis, spl...]
  transfers between devices with their start and end apart: 30 -> 30, of which waited for: 14 -> 15; matrix products, arithmetic and copies ran while one was open for 25% -> 21% of each run, Pallas kernels for 26% -> 25%
where the time goes in v2:
time: 571 us; the launch traced here: 564 us
  Pallas kernels  197 us (35%)
  waiting for transfers between devices  158 us (28%)
  other arithmetic  72.1 us (13%)
  matrix products  49.9 us (9%)
  starting transfers between devices  43 us (8%)
  local copies, waits for them, and re-layouts  29.2 us (5%)
  between operations  15.4 us (3%)
    pallas_call x3, Pallas kernels, back(): pl.pallas_call(functools.partial(back_kernel, kwidth), grid=(blocks,), in...  59.6 us
    all_to_all x1, waiting for transfers between devices, local(): lax.all_to_all(in_grad, 'dp', split_axis=0, concat_axis=0, tiled=True)  58.6 us
    dot_general x4, matrix products, weight_grad(): return jnp.einsum('std,stu->du', left, right, preferred_element_type=F32)  42.9 us
    pallas_call x1, Pallas kernels, local(): pl.pallas_call(join_kernel, grid=(seqs, wide_blocks), in_specs=[scalar_sp...  27.6 us
    ppermute x3, waiting for transfers between devices, gather_rows(): lax.ppermute(down, 'dp', [(2 * i + j, 2 * i - 2 + j) for i in range(1, 5...  26.2 us
    pallas_call x1, Pallas kernels, local(): pl.pallas_call(mix_kernel, grid=(seqs, wide_blocks), in_specs=[scalar_spe...  23.4 us
    pallas_call x1, Pallas kernels, local(): pl.pallas_call(functools.partial(project_kernel, kwidth), grid=(seqs, wid...  23.3 us
    pallas_call x1, Pallas kernels, local(): pl.pallas_call(gate_kernel, grid=(seqs, wide_blocks), in_specs=[by_rows(m...  23.2 us
  transfers between devices with their start and end apart: 30, of which 15 were waited for; matrix products, arithmetic and copies ran while one was open for 21% of the time, Pallas kernels for 25%

profile of v2, /device:TPU:0, one launch (start us, length us, event | category | flops | bytes accessed | tf_op | source)
XLA Modules:
  0.0 564.3 jit_solution(4942706337257239141)
XLA Ops:
  34.0 13.6 %collective-permute-done.5 = bf16[192,1152]{1,0:T(8,128)(2,1)S(1)} collective-permute-done((bf16[192,1152]{1,0:T(8,128)(2,1)S(1)}, bf16[192,1152]{1,0:T(8,128)(2,1)S(1)}, u32[]{:S(2)}, u32[]{:S(2)}) %collective-permute-start.5) | collective-permute-done | bytes 442400 | tf_op jit(solution)/shard_map/ppermute | solution.py:722
  49.8 9.3 %collective-permute-done.6 = bf16[192,1152]{1,0:T(8,128)(2,1)} collective-permute-done((bf16[192,1152]{1,0:T(8,128)(2,1)S(1)}, bf16[192,1152]{1,0:T(8,128)(2,1)}, u32[]{:S(2)}, u32[]{:S(2)}) %collective-permute-start.6) | collective-permute-done | bytes 442400 | tf_op jit(solution)/shard_map/ppermute | solution.py:722
  71.2 5.6 fusion
  77.4 9.6 %fusion.2.normed = bf16[3,1024,1536]{2,1,0:T(8,128)(2,1)} fusion(bf16[3,1024,1536]{2,1,0:T(8,128)(2,1)} %param.18, f32[1536]{0:T(1024)S(1)} %copy-done.16, f32[3,1024]{1,0:T(4,128)S(1)} %get-tuple-element.251), kind=kLoop, calls=%fused_computation.4 | loop fusion | flops 18874368 | bytes 18892800 | tf_op jit(solution)/shard_map/convert_element_type | solution.py:894
  87.0 22.1 %collective-permute-done.7 = bf16[576,1152]{1,0:T(8,128)(2,1)S(1)} collective-permute-done((bf16[576,1152]{1,0:T(8,128)(2,1)S(1)}, bf16[576,1152]{1,0:T(8,128)(2,1)S(1)}, u32[]{:S(2)}, u32[]{:S(2)}) %collective-permute-start.7) | collective-permute-done | bytes 1327136 | tf_op jit(solution)/shard_map/ppermute | solution.py:735
  111.5 23.3 %project.1 = (bf16[3,1024,768]{2,1,0:T(8,128)(2,1)}, f32[3,1024,256]{2,1,0:T(8,128)}, bf16[3,1024,768]{2,1,0:T(8,128)(2,1)}, bf16[3,1024,256]{2,1,0:T(8,128)(2,1...) custom-call(bf16[3,1024,1536]{2,1,0:T(8,128)(2,1)} %fusion.2.normed, ...), custom_call_target="tpu_custom_call" | custom-call | flops 700000000 | bytes 589824 | tf_op jit(solution)/shard_map/project/pallas_call | solution.py:908
  134.9 17.9 %scan.1 = (f32[3,1024,768]{2,1,0:T(8,128)}, bf16[3,8,128,768]{3,2,1,0:T(8,128)(2,1)}) custom-call(bf16[3,1024,768]{2,1,0:T(8,128)(2,1)} %get-tuple-element.88.conv_x, bf16[3,1024,256]{2,1,0:T(8,128)(2,1)S(1)} %get-tuple-element.89.conv_bc.after_bc, f32[3,1024,128]{2,1,0:T(8,128)} %get-tuple-element.90.step.after_delta, ...), custom_call_target="tpu_custom_call" | custom-call | flops 500000000 | bytes 471859 | tf_op jit(solution)/shard_map/scan/pallas_call | solution.py:945
  152.8 23.2 %gate.1 = (bf16[3,1024,768]{2,1,0:T(8,128)(2,1)}, bf16[3,1024,768]{2,1,0:T(8,128)(2,1)}, f32[3,8,1024]{2,1,0:T(8,128)S(1)}) custom-call(bf16[3,1024,1536]{2,1,0:T(8,128)(2,1)} %fusion.2.normed, bf16[3,1024,1536]{2,1,0:T(8,128)(2,1)} %cotangent.1, bf16[1536,1536]{1,0:T(8,128)(2,1)} %all-gather.2.cloned.1.call-done.weight.gate_weight, ...), custom_call_target="tpu_custom_call" | custom-call | flops 675000000 | bytes 943718 | tf_op jit(solution)/shard_map/gate/pallas_call | solution.py:970
  181.3 23.4 %mix.1 = (bf16[3,1024,768]{2,1,0:T(8,128)(2,1)}, bf16[3,1024,768]{2,1,0:T(8,128)(2,1)}, bf16[3,1024,768]{2,1,0:T(8,128)(2,1)}, bf16[2,3,1024,384]{3,2,1,0:T(8,12...) custom-call(s32[4]{0:T(128)S(1)} %add_multiply_fusion.starts, f32[3,1024,768]{2,1,0:T(8,128)} %get-tuple-element.92.y, ...), custom_call_target="tpu_custom_call" | custom-call | flops 700000000 | bytes 1061683 | tf_op jit(solution)/shard_map/mix/pallas_call | solution.py:999
  204.8 12.0 %fusion.10 = bf16[1536,768]{1,0:T(8,128)(2,1)S(1)} fusion(bf16[3,1024,768]{2,1,0:T(8,128)(2,1)} %get-tuple-element.99, bf16[3,1024,1536]{2,1,0:T(8,128)(2,1)} %cotangent.1), kind=kOutput, calls=%fused_computation.23 | convolution fusion | flops 7248936960 | bytes 16515072 | tf_op jit(solution)/shard_map/std,stu->du/dot_general | solution.py:1037
  216.8 7.9 %bitcast_convert_fusion.1 = bf16[1536,768]{1,0:T(8,128)(2,1)S(1)} fusion(bf16[3,1024,1536]{2,1,0:T(8,128)(2,1)S(1)} %bitcast.125, bf16[3,1024,768]{2,1,0:T(8,128)(2,1)S(1)} %copy-done.4), kind=kOutput, calls=%fused_computation.20 | convolution fusion | flops 7248936960 | bytes 16515072 | tf_op jit(solution)/shard_map/std,stu->du/dot_general | solution.py:1037
  233.6 20.1 %back.3 = (bf16[3,1024,768]{2,1,0:T(8,128)(2,1)}, bf16[3,1024,256]{2,1,0:T(8,128)(2,1)}, bf16[3,1024,128]{2,1,0:T(8,128)(2,1)S(1)}, f32[48,768]{1,0:T(8,128)S(1)}, f32[16,128]{1,0:T(8,128)S(1)}) custom-call(bf16[3,1024,768]{2,1,0:T(8,128)(2,1)} %get-tuple-element.88.conv_x, bf16[3,1024,256]{2,1,0:T(8,128)(2,1)} %copy-done, ...), custom_call_target="tpu_custom_call" | custom-call | flops 625000000 | bytes 314572 | tf_op jit(solution)/shard_map/back/pallas_call | solution.py:1070
  253.8 19.7 %back.4 = (bf16[3,1024,768]{2,1,0:T(8,128)(2,1)}, bf16[3,1024,256]{2,1,0:T(8,128)(2,1)}, bf16[3,1024,128]{2,1,0:T(8,128)(2,1)S(1)}, f32[48,768]{1,0:T(8,128)S(1)}, f32[16,128]{1,0:T(8,128)S(1)}) custom-call(bf16[3,1024,768]{2,1,0:T(8,128)(2,1)} %get-tuple-element.88.conv_x, ...), custom_call_target="tpu_custom_call", output_to_operand_aliasing={{3}: (14, {}), {4}: (15, {}), {0}: (16, {}), {1}: (17, {}),... | custom-call | flops 625000000 | bytes 314572 | tf_op jit(solution)/shard_map/back/pallas_call | solution.py:1070
  273.4 19.9 %back.5 = (bf16[3,1024,768]{2,1,0:T(8,128)(2,1)}, bf16[3,1024,256]{2,1,0:T(8,128)(2,1)}, bf16[3,1024,128]{2,1,0:T(8,128)(2,1)S(1)}, f32[48,768]{1,0:T(8,128)S(1)}, f32[16,128]{1,0:T(8,128)S(1)}) custom-call(bf16[3,1024,768]{2,1,0:T(8,128)(2,1)} %get-tuple-element.88.conv_x, ...), custom_call_target="tpu_custom_call", output_to_operand_aliasing={{3}: (14, {}), {4}: (15, {}), {0}: (16, {}), {1}: (17, {}),... | custom-call | flops 625000000 | bytes 314572 | tf_op jit(solution)/shard_map/back/pallas_call | solution.py:1070
  293.3 13.4 %bitcast_convert_fusion = bf16[1536,768]{1,0:T(8,128)(2,1)} fusion(bf16[3,1024,1536]{2,1,0:T(8,128)(2,1)} %fusion.2.normed, bf16[3,1024,768]{2,1,0:T(8,128)(2,1)} %get-tuple-element.128.grad_in), kind=kOutput, calls=%fused_computation.19 | convolution fusion | flops 7248936960 | bytes 16515072 | tf_op jit(solution)/shard_map/std,stu->du/dot_general | solution.py:1037
  316.9 27.6 %join.1 = (bf16[2,3,1024,384]{3,2,1,0:T(8,128)(2,1)}, bf16[2,3,1024,384]{3,2,1,0:T(8,128)(2,1)}) custom-call(s32[4]{0:T(128)S(1)} %add_multiply_fusion.starts, bf16[3,1024,768]{2,1,0:T(8,128)(2,1)} %get-tuple-element.100.grad_gate, bf16[3,1024,768]{2,1,0:T(8,128)(2,1)} %get-tuple-element.128.grad_in, ...), custom_call_target="tpu_custom_call" | custom-call | flops 825000000 | bytes 471859 | tf_op jit(solution)/shard_map/join/pallas_call | solution.py:1153
  344.5 58.6 %all-to-all-done = bf16[8,192,768]{2,1,0:T(8,128)(2,1)} async-done(((bf16[8,192,768]{2,1,0:T(8,128)(2,1)}), bf16[8,192,768]{2,1,0:T(8,128)(2,1)}, u32[]{:S(2)}, u32[]{:S(2)}) %all-to-all-start) | async-done | bytes 2359328 | tf_op jit(solution)/shard_map/all_to_all | solution.py:1150
  406.0 6.1 %collective-permute-done.17 = bf16[3,512,256]{2,1,0:T(8,128)(2,1)S(1)} collective-permute-done((bf16[3,512,256]{2,1,0:T(8,128)(2,1)S(1)}, bf16[3,512,256]{2,1,0:T(8,128)(2,1)S(1)}, u32[]{:S(2)}, u32[]{:S(2)}) %collective-permute-start.17) | collective-permute-done | bytes 786464 | tf_op jit(solution)/shard_map/ppermute | solution.py:774
  417.2 8.7 %bc_back.1 = (bf16[3,1024,384]{2,1,0:T(8,128)(2,1)}, f32[40,256]{1,0:T(8,128)S(1)}) custom-call(bf16[3,1024,256]{2,1,0:T(8,128)(2,1)} %pad_maximum_fusion.1.summed, f32[3,1024,256]{2,1,0:T(8,128)} %get-tuple-element.140.pre, f32[8,256]{1,0:T(8,128)S(1)} %slice.250.taps, bf16[3,1024,128]{2,1,0:T(8,128)(2,1)S(1)} %get-tuple-element.131.grad_delta), custom_call_target="tpu_custom_call" | custom-call | flops 200000000 | bytes 235929 | tf_op jit(solution)/shard_map/bc_back/pallas_call | solution.py:1194
  425.9 9.6 %fusion.11 = bf16[1536,384]{1,0:T(8,128)(2,1)} fusion(bf16[3,1024,1536]{2,1,0:T(8,128)(2,1)} %fusion.2.normed, bf16[3,1024,384]{2,1,0:T(8,128)(2,1)} %get-tuple-element.141), kind=kOutput, calls=%fused_computation.25 | convolution fusion | flops 3624468480 | bytes 12976128 | tf_op jit(solution)/shard_map/std,stu->du/dot_general | solution.py:1037
  462.0 13.4 %all-to-all-done.1 = bf16[8,192,384]{2,1,0:T(8,128)(2,1)} async-done(((bf16[8,192,384]{2,1,0:T(8,128)(2,1)}), bf16[8,192,384]{2,1,0:T(8,128)(2,1)}, u32[]{:S(2)}, u32[]{:S(2)}) %all-to-all-start.1) | async-done | bytes 1179680 | tf_op jit(solution)/shard_map/all_to_all | solution.py:1212
  486.2 10.6 %collective-permute-done.18 = bf16[3,1024,384]{2,1,0:T(8,128)(2,1)} collective-permute-done((bf16[3,1024,384]{2,1,0:T(8,128)(2,1)}, bf16[3,1024,384]{2,1,0:T(8,128)(2,1)}, u32[]{:S(2)}, u32[]{:S(2)}) %collective-permute-start.18) | collective-permute-done | bytes 2359328 | tf_op jit(solution)/shard_map/ppermute | solution.py:667
  496.9 7.0 %fusion.6 = (f32[3,1024]{1,0:T(4,128)S(1)}, f32[384]{0:T(512)S(1)}, f32[3,1024,384]{2,1,0:T(8,128)}) fusion(f32[384]{0:T(512)S(1)} %dynamic_slice.35, bf16[3,1024,1536]{2,1,0:T(8,128)(2,1)} %param.18, s32[]{:T(128)S(6)} %select_n.148, f32[3,1024]{1,0:T(4,128)S(1)} %get-tuple-element.251, ...), kind=kOutput, calls=%fused_computation.12 | convolution fusion | flops 619311744 | bytes 15952904 | tf_op jit(solution)/shard_map/btk,fk->btf/dot_general | solution.py:1239
  529.2 9.0 %fusion.5 = (f32[3,1024,384]{2,1,0:T(8,128)}, bf16[3,1024,384]{2,1,0:T(8,128)(2,1)}) fusion(f32[3,1024,384]{2,1,0:T(8,128)} %get-tuple-element.252, f32[3,1024]{1,0:T(4,128)S(1)} %div.65, f32[3,1024]{1,0:T(4,128)} %get-tuple-element.250, f32[384]{0:T(512)} %copy-done.20, f32[3,1024]{1,0:T(4,128)S(1)} %get-tuple-element.251, ...), kind=kLoop, calls=%fused_computation.11 | loop fusion | flops 14155776 | bytes 21272068 | tf_op jit(solution)/shard_map/sub | solution.py:1256
  (228 shorter events, 157.2 us)
Async XLA Ops:
  7.2 145.6 %all-gather.2.cloned.1.call-start = ((), (), s32[]{:S(2)}) async-start(), calls=%async_computation.5 | async-start | bytes 5308416 | tf_op jit(solution)/shard_map/all_gather | solution.py:889
  13.6 13.1 %collective-permute-start.2 = (bf16[192,1152]{1,0:T(8,128)(2,1)S(1)}, bf16[192,1152]{1,0:T(8,128)(2,1)S(1)}, u32[]{:S(2)}, u32[]{:S(2)}) collective-permute-start(bf16[192,1152]{1,0:T(8,128)(2,1)S(1)} %get-tuple-element.247), channel_id=1, source_target_pairs={{0,4},{4,0},{8,12},{12,8},{16,20},{20,16},{24,28},{28,24},{1,5},{5... | collective-permute-start | bytes 1327112 | tf_op jit(solution)/shard_map/ppermute | solution.py:715
  16.6 13.5 %collective-permute-start.1 = (bf16[192,1152]{1,0:T(8,128)(2,1)S(1)}, bf16[192,1152]{1,0:T(8,128)(2,1)S(1)}, u32[]{:S(2)}, u32[]{:S(2)}) collective-permute-start(bf16[192,1152]{1,0:T(8,128)(2,1)S(1)} %get-tuple-element.247), channel_id=1, source_target_pairs={{8,0},{12,4},{16,8},{20,12},{24,16},{28,20},{9,1},{13,5},{17,9},{2... | collective-permute-start | bytes 1327112 | tf_op jit(solution)/shard_map/ppermute | solution.py:722
  17.9 13.4 %collective-permute-start = (bf16[192,1152]{1,0:T(8,128)(2,1)S(1)}, bf16[192,1152]{1,0:T(8,128)(2,1)S(1)}, u32[]{:S(2)}, u32[]{:S(2)}) collective-permute-start(bf16[192,1152]{1,0:T(8,128)(2,1)S(1)} %get-tuple-element.247), channel_id=1, source_target_pairs={{0,8},{4,12},{8,16},{12,20},{16,24},{20,28},{1,9},{5,13},{9,17},{1... | collective-permute-start | bytes 1327112 | tf_op jit(solution)/shard_map/ppermute | solution.py:719
  32.0 15.6 %collective-permute-start.5 = (bf16[192,1152]{1,0:T(8,128)(2,1)S(1)}, bf16[192,1152]{1,0:T(8,128)(2,1)S(1)}, u32[]{:S(2)}, u32[]{:S(2)}) collective-permute-start(bf16[192,1152]{1,0:T(8,128)(2,1)S(1)} %collective-permute-done.1), channel_id=1, source_target_pairs={{8,0},{12,4},{16,8},{20,12},{9,1},{13,5},{17,9},{21,13},{10,2},{14... | collective-permute-start | bytes 1327112 | tf_op jit(solution)/shard_map/ppermute | solution.py:722
  33.3 16.5 %collective-permute-start.4 = (bf16[192,1152]{1,0:T(8,128)(2,1)S(1)}, bf16[192,1152]{1,0:T(8,128)(2,1)S(1)}, u32[]{:S(2)}, u32[]{:S(2)}) collective-permute-start(bf16[192,1152]{1,0:T(8,128)(2,1)S(1)} %collective-permute-done.3), channel_id=1, source_target_pairs={{16,24},{20,28},{17,25},{21,29},{18,26},{22,30},{19,27},{23,31}} | collective-permute-start | bytes 1327112 | tf_op jit(solution)/shard_map/ppermute | solution.py:719
  47.6 11.5 %collective-permute-start.6 = (bf16[192,1152]{1,0:T(8,128)(2,1)S(1)}, bf16[192,1152]{1,0:T(8,128)(2,1)}, u32[]{:S(2)}, u32[]{:S(2)}) collective-permute-start(bf16[192,1152]{1,0:T(8,128)(2,1)S(1)} %collective-permute-done.5), channel_id=1, source_target_pairs={{8,0},{12,4},{9,1},{13,5},{10,2},{14,6},{11,3},{15,7}} | collective-permute-start | bytes 1327112 | tf_op jit(solution)/shard_map/ppermute | solution.py:722
  70.5 38.6 %collective-permute-start.7 = (bf16[576,1152]{1,0:T(8,128)(2,1)S(1)}, bf16[576,1152]{1,0:T(8,128)(2,1)S(1)}, u32[]{:S(2)}, u32[]{:S(2)}) collective-permute-start(bf16[576,1152]{1,0:T(8,128)(2,1)S(1)} %pad_maximum_fusion.2), channel_id=1, source_target_pairs={{0,4},{4,0},{8,12},{12,8},{16,20},{20,16},{24,28},{28,24},{1,5},{5... | collective-permute-start | bytes 3981320 | tf_op jit(solution)/shard_map/ppermute | solution.py:735
  204.7 22.4 %collective-permute-start.10 = (bf16[2,3,1024,384]{3,2,1,0:T(8,128)(2,1)}, bf16[2,3,1024,384]{3,2,1,0:T(8,128)(2,1)}, u32[]{:S(2)}, u32[]{:S(2)}) collective-permute-start(bf16[2,3,1024,384]{3,2,1,0:T(8,128)(2,1)} %get-tuple-element.104), channel_id=1, source_target_pairs={{0,1},{1,0},{2,3},{3,2},{4,5},{5,4},{6,7},{7,6},{8,9},{9,8},{10,11... | collective-permute-start | bytes 14155784 | tf_op jit(solution)/shard_map/ppermute | solution.py:1132
  230.1 63.2 %collective-permute-start.11 = (bf16[1024,384]{1,0:T(8,128)(2,1)S(1)}, bf16[1024,384]{1,0:T(8,128)(2,1)S(1)}, u32[]{:S(2)}, u32[]{:S(2)}) collective-permute-start(bf16[1024,384]{1,0:T(8,128)(2,1)S(1)} %get-tuple-element.122), channel_id=1, source_target_pairs={{0,2},{1,3},{2,0},{3,1},{4,6},{5,7},{6,4},{7,5},{8,10},{9,11},{10,... | collective-permute-start | bytes 2359304 | tf_op jit(solution)/shard_map/ppermute | solution.py:667
  231.6 61.7 %collective-permute-start.12 = (bf16[1024,384]{1,0:T(8,128)(2,1)S(1)}, bf16[1024,384]{1,0:T(8,128)(2,1)S(1)}, u32[]{:S(2)}, u32[]{:S(2)}) collective-permute-start(bf16[1024,384]{1,0:T(8,128)(2,1)S(1)} %get-tuple-element.123), channel_id=1, source_target_pairs={{0,2},{1,3},{2,0},{3,1},{4,6},{5,7},{6,4},{7,5},{8,10},{9,11},{10,... | collective-permute-start | bytes 2359304 | tf_op jit(solution)/shard_map/ppermute | solution.py:667
  232.1 61.2 %collective-permute-start.13 = (bf16[1024,384]{1,0:T(8,128)(2,1)S(1)}, bf16[1024,384]{1,0:T(8,128)(2,1)S(1)}, u32[]{:S(2)}, u32[]{:S(2)}) collective-permute-start(bf16[1024,384]{1,0:T(8,128)(2,1)S(1)} %get-tuple-element.124), channel_id=1, source_target_pairs={{0,2},{1,3},{2,0},{3,1},{4,6},{5,7},{6,4},{7,5},{8,10},{9,11},{10,... | collective-permute-start | bytes 2359304 | tf_op jit(solution)/shard_map/ppermute | solution.py:667
  306.8 96.4 %all-to-all-start = ((bf16[8,192,768]{2,1,0:T(8,128)(2,1)}), bf16[8,192,768]{2,1,0:T(8,128)(2,1)}, u32[]{:S(2)}, u32[]{:S(2)}) async-start(bf16[8,192,768]{2,1,0:T(8,128)(2,1)} %bitcast.126), calls=%async_computation | async-start | bytes 4718592 | tf_op jit(solution)/shard_map/all_to_all | solution.py:1150
  311.3 143.1 %reduce-scatter.2.cloned.1.call-start = ((), (), s32[]{:S(2)}) async-start(), calls=%async_computation.6 | async-start | bytes 5308416 | tf_op jit(solution)/shard_map/reduce_scatter | solution.py:1044
  316.3 28.2 %collective-permute-start.15 = (bf16[3,512,256]{2,1,0:T(8,128)(2,1)S(1)}, bf16[3,512,256]{2,1,0:T(8,128)(2,1)S(1)}, u32[]{:S(2)}, u32[]{:S(2)}) collective-permute-start(bf16[3,512,256]{2,1,0:T(8,128)(2,1)S(1)} %add_convert_fusion.2), channel_id=1, source_target_pairs={{0,2},{1,3},{2,0},{3,1},{4,6},{5,7},{6,4},{7,5},{8,10},{9,11},{10,... | collective-permute-start | bytes 2359304 | tf_op jit(solution)/shard_map/ppermute | solution.py:764
  403.1 10.4 %collective-permute-start.16 = (bf16[2,3,1024,384]{3,2,1,0:T(8,128)(2,1)}, bf16[2,3,1024,384]{3,2,1,0:T(8,128)(2,1)}, u32[]{:S(2)}, u32[]{:S(2)}) collective-permute-start(bf16[2,3,1024,384]{3,2,1,0:T(8,128)(2,1)} %get-tuple-element.136), channel_id=1, source_target_pairs={{0,1},{1,0},{2,3},{3,2},{4,5},{5,4},{6,7},{7,6},{8,9},{9,8},{10,11... | collective-permute-start | bytes 14155784 | tf_op jit(solution)/shard_map/ppermute | solution.py:1182
  404.5 7.7 %collective-permute-start.17 = (bf16[3,512,256]{2,1,0:T(8,128)(2,1)S(1)}, bf16[3,512,256]{2,1,0:T(8,128)(2,1)S(1)}, u32[]{:S(2)}, u32[]{:S(2)}) collective-permute-start(bf16[3,512,256]{2,1,0:T(8,128)(2,1)S(1)} %add_convert_fusion.1), channel_id=1, source_target_pairs={{0,1},{1,0},{2,3},{3,2},{4,5},{5,4},{6,7},{7,6},{8,9},{9,8},{10,11... | collective-permute-start | bytes 2359304 | tf_op jit(solution)/shard_map/ppermute | solution.py:774
  435.5 39.9 %all-to-all-start.1 = ((bf16[8,192,384]{2,1,0:T(8,128)(2,1)}), bf16[8,192,384]{2,1,0:T(8,128)(2,1)}, u32[]{:S(2)}, u32[]{:S(2)}) async-start(bf16[8,192,384]{2,1,0:T(8,128)(2,1)} %bitcast.27), calls=%async_computation.2 | async-start | bytes 2359296 | tf_op jit(solution)/shard_map/all_to_all | solution.py:1212
  443.2 53.7 %collective-permute-start.18 = (bf16[3,1024,384]{2,1,0:T(8,128)(2,1)}, bf16[3,1024,384]{2,1,0:T(8,128)(2,1)}, u32[]{:S(2)}, u32[]{:S(2)}) collective-permute-start(bf16[3,1024,384]{2,1,0:T(8,128)(2,1)} %fusion.12), channel_id=1, source_target_pairs={{0,2},{1,3},{2,0},{3,1},{4,6},{5,7},{6,4},{7,5},{8,10},{9,11},{10,... | collective-permute-start | bytes 7077896 | tf_op jit(solution)/shard_map/ppermute | solution.py:667
  482.3 28.0 %all-to-all-start.2 = ((f32[24,64,128]{2,1,0:T(8,128)}), f32[24,64,128]{2,1,0:T(8,128)S(1)}, u32[]{:S(2)}, u32[]{:S(2)}) async-start(f32[24,64,128]{2,1,0:T(8,128)} %shard_map.313), calls=%async_computation.3 | async-start | bytes 1572864 | tf_op jit(solution)/shard_map/all_to_all | solution.py:814
  514.6 5.6 collective-permute-start.21
  520.2 6.0 %collective-permute-start.22 = (f32[7460]{0:T(1024)S(1)}, f32[7460]{0:T(1024)S(1)}, u32[]{:S(2)}, u32[]{:S(2)}) collective-permute-start(f32[7460]{0:T(1024)S(1)} %add.424), channel_id=1, source_target_pairs={{0,8},{4,12},{8,0},{12,4},{16,24},{20,28},{24,16},{28,20},{1,9},{5... | collective-permute-start | bytes 89528 | tf_op jit(solution)/shard_map/ppermute | solution.py:785
  522.6 21.3 %all-to-all-start.3 = ((bf16[8,3,64,128]{3,2,1,0:T(8,128)(2,1)}), bf16[8,3,64,128]{3,2,1,0:T(8,128)(2,1)S(1)}, u32[]{:S(2)}, u32[]{:S(2)}) async-start(bf16[8,3,64,128]{3,2,1,0:T(8,128)(2,1)} %broadcast_in_dim.57), calls=%async_computation.4 | async-start | bytes 786432 | tf_op jit(solution)/shard_map/all_to_all | solution.py:635
  526.2 12.0 %collective-permute-start.23 = (f32[7460]{0:T(1024)S(1)}, f32[7460]{0:T(1024)S(1)}, u32[]{:S(2)}, u32[]{:S(2)}) collective-permute-start(f32[7460]{0:T(1024)S(1)} %add.425), channel_id=1, source_target_pairs={{0,16},{4,20},{8,24},{12,28},{16,0},{20,4},{24,8},{28,12},{1,17},{... | collective-permute-start | bytes 89528 | tf_op jit(solution)/shard_map/ppermute | solution.py:785
  (33 other events, 613.7 us)
Sparse Core Ops, SparseCore 0:
  59.2 83.4 all-gather.1
  315.8 138.5 reduce-scatter.1

commit v3 on v2

--- a/solution.py
+++ b/solution.py
@@ -1176,13 +1176,11 @@
         first_weight,
         first_weight,
     )
-    normed_own, normed_other, bc_moved, in_parts = tie(
-        normed_own, normed_other, bc_moved, in_parts
-    )
+    normed_other, bc_moved = tie(normed_other, bc_moved)
     normed_arrived = lax.ppermute(normed_other, "tensor", [(i, i ^ 1) for i in range(tensor)])
     normed_kept, normed_leaving = core_sums(normed_own, normed_arrived)
     bc_total = finish_total(bc_chip, bc_moved)
-    bc_total, *normed_leaving = tie(bc_total, *normed_leaving)
+    bc_total, in_parts, *normed_leaving = tie(bc_total, in_parts, *normed_leaving)
     normed_moved = column_sends(normed_leaving)
     out_sums = []
     for kept, moved in zip(out_kept, arrivals):

time: 571 us -> 549 us (0.961)
  waiting for transfers between devices: 158 us -> 131 us
    all_to_all x1, waiting for transfers between devices: 58.6 us -> 43.3 us  [local(): lax.all_to_all(in_grad, 'dp', split_axis=0, concat_axis=0, tiled=True)]
    ppermute x4, waiting for transfers between devices: 10.6 us -> 17.1 us  [column_sends(): lax.ppermute(sent, 'tensor', [(i, (i // 2 + shift) % columns * 2 + i % 2)...]
  transfers between devices with their start and end apart: 30 -> 30, of which waited for: 15 -> 13; matrix products, arithmetic and copies ran while one was open for 21% -> 24% of each run, Pallas kernels for 25% -> 26%
where the time goes in v3:
time: 549 us; the launch traced here: 542 us
  Pallas kernels  197 us (36%)
  waiting for transfers between devices  131 us (24%)
  other arithmetic  73.9 us (13%)
  matrix products  49.2 us (9%)
  starting transfers between devices  45.6 us (8%)
  local copies, waits for them, and re-layouts  30.6 us (6%)
  between operations  15.4 us (3%)
    pallas_call x3, Pallas kernels, back(): pl.pallas_call(functools.partial(back_kernel, kwidth), grid=(blocks,), in...  59.7 us
    all_to_all x1, waiting for transfers between devices, local(): lax.all_to_all(in_grad, 'dp', split_axis=0, concat_axis=0, tiled=True)  43.3 us
    dot_general x4, matrix products, weight_grad(): return jnp.einsum('std,stu->du', left, right, preferred_element_type=F32)  42.3 us
    pallas_call x1, Pallas kernels, local(): pl.pallas_call(join_kernel, grid=(seqs, wide_blocks), in_specs=[scalar_sp...  27.4 us
    ppermute x3, waiting for transfers between devices, gather_rows(): lax.ppermute(down, 'dp', [(2 * i + j, 2 * i - 2 + j) for i in range(1, 5...  26.3 us
    pallas_call x1, Pallas kernels, local(): pl.pallas_call(mix_kernel, grid=(seqs, wide_blocks), in_specs=[scalar_spe...  23.4 us
    pallas_call x1, Pallas kernels, local(): pl.pallas_call(functools.partial(project_kernel, kwidth), grid=(seqs, wid...  23.4 us
    pallas_call x1, Pallas kernels, local(): pl.pallas_call(gate_kernel, grid=(seqs, wide_blocks), in_specs=[by_rows(m...  23.2 us
  transfers between devices with their start and end apart: 30, of which 13 were waited for; matrix products, arithmetic and copies ran while one was open for 24% of the time, Pallas kernels for 26%

profile of v3, /device:TPU:0, one launch (start us, length us, event | category | flops | bytes accessed | tf_op | source)
XLA Modules:
  0.0 542.4 jit_solution(6344040112282850492)
XLA Ops:
  34.0 13.6 %collective-permute-done.5 = bf16[192,1152]{1,0:T(8,128)(2,1)S(1)} collective-permute-done((bf16[192,1152]{1,0:T(8,128)(2,1)S(1)}, bf16[192,1152]{1,0:T(8,128)(2,1)S(1)}, u32[]{:S(2)}, u32[]{:S(2)}) %collective-permute-start.5) | collective-permute-done | bytes 442400 | tf_op jit(solution)/shard_map/ppermute | solution.py:722
  49.8 9.3 %collective-permute-done.6 = bf16[192,1152]{1,0:T(8,128)(2,1)} collective-permute-done((bf16[192,1152]{1,0:T(8,128)(2,1)S(1)}, bf16[192,1152]{1,0:T(8,128)(2,1)}, u32[]{:S(2)}, u32[]{:S(2)}) %collective-permute-start.6) | collective-permute-done | bytes 442400 | tf_op jit(solution)/shard_map/ppermute | solution.py:722
  71.2 5.6 %fusion = f32[3,1024]{1,0:T(4,128)S(1)} fusion(bf16[3,1024,1536]{2,1,0:T(8,128)(2,1)} %param.18), kind=kLoop, calls=%fused_computation.2 | loop fusion | flops 14152704 | bytes 9449472 | tf_op jit(solution)/shard_map/reduce_sum | solution.py:893
  77.5 9.6 %fusion.2.normed = bf16[3,1024,1536]{2,1,0:T(8,128)(2,1)} fusion(bf16[3,1024,1536]{2,1,0:T(8,128)(2,1)} %param.18, f32[1536]{0:T(1024)S(1)} %copy-done.14, f32[3,1024]{1,0:T(4,128)S(1)} %get-tuple-element.249), kind=kLoop, calls=%fused_computation.4 | loop fusion | flops 18874368 | bytes 18892800 | tf_op jit(solution)/shard_map/convert_element_type | solution.py:894
  87.1 22.2 %collective-permute-done.7 = bf16[576,1152]{1,0:T(8,128)(2,1)S(1)} collective-permute-done((bf16[576,1152]{1,0:T(8,128)(2,1)S(1)}, bf16[576,1152]{1,0:T(8,128)(2,1)S(1)}, u32[]{:S(2)}, u32[]{:S(2)}) %collective-permute-start.7) | collective-permute-done | bytes 1327136 | tf_op jit(solution)/shard_map/ppermute | solution.py:735
  111.7 23.4 %project.1 = (bf16[3,1024,768]{2,1,0:T(8,128)(2,1)}, f32[3,1024,256]{2,1,0:T(8,128)}, bf16[3,1024,768]{2,1,0:T(8,128)(2,1)}, bf16[3,1024,256]{2,1,0:T(8,128)(2,1...) custom-call(bf16[3,1024,1536]{2,1,0:T(8,128)(2,1)} %fusion.2.normed, ...), custom_call_target="tpu_custom_call" | custom-call | flops 700000000 | bytes 589824 | tf_op jit(solution)/shard_map/project/pallas_call | solution.py:908
  135.0 18.1 %scan.1 = (f32[3,1024,768]{2,1,0:T(8,128)}, bf16[3,8,128,768]{3,2,1,0:T(8,128)(2,1)}) custom-call(bf16[3,1024,768]{2,1,0:T(8,128)(2,1)} %get-tuple-element.87.conv_x, bf16[3,1024,256]{2,1,0:T(8,128)(2,1)S(1)} %get-tuple-element.88.conv_bc.after_bc, f32[3,1024,128]{2,1,0:T(8,128)} %get-tuple-element.89.step.after_delta, ...), custom_call_target="tpu_custom_call" | custom-call | flops 500000000 | bytes 471859 | tf_op jit(solution)/shard_map/scan/pallas_call | solution.py:945
  153.2 23.2 %gate.1 = (bf16[3,1024,768]{2,1,0:T(8,128)(2,1)}, bf16[3,1024,768]{2,1,0:T(8,128)(2,1)}, f32[3,8,1024]{2,1,0:T(8,128)S(1)}) custom-call(bf16[3,1024,1536]{2,1,0:T(8,128)(2,1)} %fusion.2.normed, bf16[3,1024,1536]{2,1,0:T(8,128)(2,1)} %cotangent.1, bf16[1536,1536]{1,0:T(8,128)(2,1)} %all-gather.2.cloned.1.call-done.weight.gate_weight, ...), custom_call_target="tpu_custom_call" | custom-call | flops 675000000 | bytes 943718 | tf_op jit(solution)/shard_map/gate/pallas_call | solution.py:970
  181.7 23.4 %mix.1 = (bf16[3,1024,768]{2,1,0:T(8,128)(2,1)}, bf16[3,1024,768]{2,1,0:T(8,128)(2,1)}, bf16[3,1024,768]{2,1,0:T(8,128)(2,1)}, bf16[2,3,1024,384]{3,2,1,0:T(8,12...) custom-call(s32[4]{0:T(128)S(1)} %add_multiply_fusion.starts, f32[3,1024,768]{2,1,0:T(8,128)} %get-tuple-element.91.y, ...), custom_call_target="tpu_custom_call" | custom-call | flops 700000000 | bytes 1061683 | tf_op jit(solution)/shard_map/mix/pallas_call | solution.py:999
  205.1 12.0 %fusion.10 = bf16[1536,768]{1,0:T(8,128)(2,1)S(1)} fusion(bf16[3,1024,768]{2,1,0:T(8,128)(2,1)} %get-tuple-element.98, bf16[3,1024,1536]{2,1,0:T(8,128)(2,1)} %cotangent.1), kind=kOutput, calls=%fused_computation.23 | convolution fusion | flops 7248936960 | bytes 16515072 | tf_op jit(solution)/shard_map/std,stu->du/dot_general | solution.py:1037
  217.2 7.9 %bitcast_convert_fusion.1 = bf16[1536,768]{1,0:T(8,128)(2,1)S(1)} fusion(bf16[3,1024,1536]{2,1,0:T(8,128)(2,1)S(1)} %bitcast.125, bf16[3,1024,768]{2,1,0:T(8,128)(2,1)S(1)} %copy-done.4), kind=kOutput, calls=%fused_computation.20 | convolution fusion | flops 7248936960 | bytes 16515072 | tf_op jit(solution)/shard_map/std,stu->du/dot_general | solution.py:1037
  235.2 20.1 %back.3 = (bf16[3,1024,768]{2,1,0:T(8,128)(2,1)}, bf16[3,1024,256]{2,1,0:T(8,128)(2,1)}, bf16[3,1024,128]{2,1,0:T(8,128)(2,1)S(1)}, f32[48,768]{1,0:T(8,128)S(1)}, f32[16,128]{1,0:T(8,128)S(1)}) custom-call(bf16[3,1024,768]{2,1,0:T(8,128)(2,1)} %get-tuple-element.87.conv_x, bf16[3,1024,256]{2,1,0:T(8,128)(2,1)} %copy-done, ...), custom_call_target="tpu_custom_call" | custom-call | flops 625000000 | bytes 314572 | tf_op jit(solution)/shard_map/back/pallas_call | solution.py:1070
  255.3 19.7 %back.4 = (bf16[3,1024,768]{2,1,0:T(8,128)(2,1)}, bf16[3,1024,256]{2,1,0:T(8,128)(2,1)}, bf16[3,1024,128]{2,1,0:T(8,128)(2,1)S(1)}, f32[48,768]{1,0:T(8,128)S(1)}, f32[16,128]{1,0:T(8,128)S(1)}) custom-call(bf16[3,1024,768]{2,1,0:T(8,128)(2,1)} %get-tuple-element.87.conv_x, ...), custom_call_target="tpu_custom_call", output_to_operand_aliasing={{3}: (14, {}), {4}: (15, {}), {0}: (16, {}), {1}: (17, {}),... | custom-call | flops 625000000 | bytes 314572 | tf_op jit(solution)/shard_map/back/pallas_call | solution.py:1070
  275.0 19.9 %back.5 = (bf16[3,1024,768]{2,1,0:T(8,128)(2,1)}, bf16[3,1024,256]{2,1,0:T(8,128)(2,1)}, bf16[3,1024,128]{2,1,0:T(8,128)(2,1)S(1)}, f32[48,768]{1,0:T(8,128)S(1)}, f32[16,128]{1,0:T(8,128)S(1)}) custom-call(bf16[3,1024,768]{2,1,0:T(8,128)(2,1)} %get-tuple-element.87.conv_x, ...), custom_call_target="tpu_custom_call", output_to_operand_aliasing={{3}: (14, {}), {4}: (15, {}), {0}: (16, {}), {1}: (17, {}),... | custom-call | flops 625000000 | bytes 314572 | tf_op jit(solution)/shard_map/back/pallas_call | solution.py:1070
  295.0 13.2 %bitcast_convert_fusion = bf16[1536,768]{1,0:T(8,128)(2,1)} fusion(bf16[3,1024,1536]{2,1,0:T(8,128)(2,1)} %fusion.2.normed, bf16[3,1024,768]{2,1,0:T(8,128)(2,1)} %get-tuple-element.127.grad_in), kind=kOutput, calls=%fused_computation.19 | convolution fusion | flops 7248936960 | bytes 16515072 | tf_op jit(solution)/shard_map/std,stu->du/dot_general | solution.py:1037
  309.0 27.4 %join.1 = (bf16[2,3,1024,384]{3,2,1,0:T(8,128)(2,1)}, bf16[2,3,1024,384]{3,2,1,0:T(8,128)(2,1)}) custom-call(s32[4]{0:T(128)S(1)} %add_multiply_fusion.starts, bf16[3,1024,768]{2,1,0:T(8,128)(2,1)} %get-tuple-element.99.grad_gate, bf16[3,1024,768]{2,1,0:T(8,128)(2,1)} %get-tuple-element.127.grad_in, bf16[3,1024,128]{2,1,0:T(8,128)(2,1)S(1)} %get-tuple-element.130.grad_delta, ...), custom_call_target="tpu_custom_call" | custom-call | flops 825000000 | bytes 471859 | tf_op jit(solution)/shard_map/join/pallas_call | solution.py:1153
  353.3 43.3 %all-to-all-done = bf16[8,192,768]{2,1,0:T(8,128)(2,1)} async-done(((bf16[8,192,768]{2,1,0:T(8,128)(2,1)}), bf16[8,192,768]{2,1,0:T(8,128)(2,1)}, u32[]{:S(2)}, u32[]{:S(2)}) %all-to-all-start) | async-done | bytes 2359328 | tf_op jit(solution)/shard_map/all_to_all | solution.py:1150
  396.7 8.7 %bc_back.1 = (bf16[3,1024,384]{2,1,0:T(8,128)(2,1)}, f32[40,256]{1,0:T(8,128)S(1)}) custom-call(bf16[3,1024,256]{2,1,0:T(8,128)(2,1)} %pad_maximum_fusion.1.summed, f32[3,1024,256]{2,1,0:T(8,128)} %get-tuple-element.138.pre, f32[8,256]{1,0:T(8,128)S(1)} %slice.250.taps, bf16[3,1024,128]{2,1,0:T(8,128)(2,1)S(1)} %get-tuple-element.130.grad_delta), custom_call_target="tpu_custom_call" | custom-call | flops 200000000 | bytes 235929 | tf_op jit(solution)/shard_map/bc_back/pallas_call | solution.py:1192
  405.3 9.2 %fusion.11 = bf16[1536,384]{1,0:T(8,128)(2,1)} fusion(bf16[3,1024,1536]{2,1,0:T(8,128)(2,1)} %fusion.2.normed, bf16[3,1024,384]{2,1,0:T(8,128)(2,1)} %get-tuple-element.139), kind=kOutput, calls=%fused_computation.25 | convolution fusion | flops 3624468480 | bytes 12976128 | tf_op jit(solution)/shard_map/std,stu->du/dot_general | solution.py:1037
  424.5 5.5 %fusion.15 = (f32[1,1024,384]{2,1,0:T(8,128)S(1)}, f32[1,1024,384]{2,1,0:T(8,128)}, f32[1,1024,384]{2,1,0:T(8,128)}) fusion(bf16[1024,384]{1,0:T(8,128)(2,1)} %copy-done.9, bf16[2,3,1024,384]{3,2,1,0:T(8,128)(2,1)} %collective-permute-done.10, bf16[2,3,1024,384]{3,2,1,0:T(8,128)(2,1)} %get-tuple-element.104, bf16[1024,384]{1,0:T(8,128)(2,1)} %collective-permute-done.13, ...), kind=kLoop, calls=%fused_computation.34 | loop fusion | flops 5898240 | bytes 11796480 | tf_op jit(solution)/shard_map/stack | solution.py:1190
  437.7 9.5 %all-to-all-done.1 = bf16[8,192,384]{2,1,0:T(8,128)(2,1)} async-done(((bf16[8,192,384]{2,1,0:T(8,128)(2,1)}), bf16[8,192,384]{2,1,0:T(8,128)(2,1)}, u32[]{:S(2)}, u32[]{:S(2)}) %all-to-all-start.1) | async-done | bytes 1179680 | tf_op jit(solution)/shard_map/all_to_all | solution.py:1210
  458.0 17.1 %collective-permute-done.18 = bf16[3,1024,384]{2,1,0:T(8,128)(2,1)} collective-permute-done((bf16[3,1024,384]{2,1,0:T(8,128)(2,1)}, bf16[3,1024,384]{2,1,0:T(8,128)(2,1)}, u32[]{:S(2)}, u32[]{:S(2)}) %collective-permute-start.18) | collective-permute-done | bytes 2359328 | tf_op jit(solution)/shard_map/ppermute | solution.py:667
  475.1 7.0 %fusion.6 = (f32[3,1024]{1,0:T(4,128)S(1)}, f32[384]{0:T(512)S(1)}, f32[3,1024,384]{2,1,0:T(8,128)}) fusion(f32[384]{0:T(512)S(1)} %copy-done.18, bf16[3,1024,1536]{2,1,0:T(8,128)(2,1)} %param.18, s32[]{:T(128)S(6)} %select_n.148, f32[3,1024]{1,0:T(4,128)S(1)} %get-tuple-element.249, ...), kind=kOutput, calls=%fused_computation.12 | convolution fusion | flops 619311744 | bytes 15952904 | tf_op jit(solution)/shard_map/btk,fk->btf/dot_general | solution.py:1237
  507.4 9.0 %fusion.5 = (f32[3,1024,384]{2,1,0:T(8,128)}, bf16[3,1024,384]{2,1,0:T(8,128)(2,1)}) fusion(f32[3,1024,384]{2,1,0:T(8,128)} %get-tuple-element.250, f32[3,1024]{1,0:T(4,128)S(1)} %div.65, f32[3,1024]{1,0:T(4,128)} %get-tuple-element.248, f32[384]{0:T(512)} %dynamic_slice.35, f32[3,1024]{1,0:T(4,128)S(1)} %get-tuple-element.249, ...), kind=kLoop, calls=%fused_computation.11 | loop fusion | flops 14155776 | bytes 21272068 | tf_op jit(solution)/shard_map/sub | solution.py:1254
  (224 shorter events, 149.2 us)
Async XLA Ops:
  7.2 146.0 %all-gather.2.cloned.1.call-start = ((), (), s32[]{:S(2)}) async-start(), calls=%async_computation.5 | async-start | bytes 5308416 | tf_op jit(solution)/shard_map/all_gather | solution.py:889
  13.6 13.1 %collective-permute-start.2 = (bf16[192,1152]{1,0:T(8,128)(2,1)S(1)}, bf16[192,1152]{1,0:T(8,128)(2,1)S(1)}, u32[]{:S(2)}, u32[]{:S(2)}) collective-permute-start(bf16[192,1152]{1,0:T(8,128)(2,1)S(1)} %get-tuple-element.245), channel_id=1, source_target_pairs={{0,4},{4,0},{8,12},{12,8},{16,20},{20,16},{24,28},{28,24},{1,5},{5... | collective-permute-start | bytes 1327112 | tf_op jit(solution)/shard_map/ppermute | solution.py:715
  16.6 13.5 %collective-permute-start.1 = (bf16[192,1152]{1,0:T(8,128)(2,1)S(1)}, bf16[192,1152]{1,0:T(8,128)(2,1)S(1)}, u32[]{:S(2)}, u32[]{:S(2)}) collective-permute-start(bf16[192,1152]{1,0:T(8,128)(2,1)S(1)} %get-tuple-element.245), channel_id=1, source_target_pairs={{8,0},{12,4},{16,8},{20,12},{24,16},{28,20},{9,1},{13,5},{17,9},{2... | collective-permute-start | bytes 1327112 | tf_op jit(solution)/shard_map/ppermute | solution.py:722
  17.9 13.4 %collective-permute-start = (bf16[192,1152]{1,0:T(8,128)(2,1)S(1)}, bf16[192,1152]{1,0:T(8,128)(2,1)S(1)}, u32[]{:S(2)}, u32[]{:S(2)}) collective-permute-start(bf16[192,1152]{1,0:T(8,128)(2,1)S(1)} %get-tuple-element.245), channel_id=1, source_target_pairs={{0,8},{4,12},{8,16},{12,20},{16,24},{20,28},{1,9},{5,13},{9,17},{1... | collective-permute-start | bytes 1327112 | tf_op jit(solution)/shard_map/ppermute | solution.py:719
  32.0 15.6 %collective-permute-start.5 = (bf16[192,1152]{1,0:T(8,128)(2,1)S(1)}, bf16[192,1152]{1,0:T(8,128)(2,1)S(1)}, u32[]{:S(2)}, u32[]{:S(2)}) collective-permute-start(bf16[192,1152]{1,0:T(8,128)(2,1)S(1)} %collective-permute-done.1), channel_id=1, source_target_pairs={{8,0},{12,4},{16,8},{20,12},{9,1},{13,5},{17,9},{21,13},{10,2},{14... | collective-permute-start | bytes 1327112 | tf_op jit(solution)/shard_map/ppermute | solution.py:722
  33.3 16.5 %collective-permute-start.4 = (bf16[192,1152]{1,0:T(8,128)(2,1)S(1)}, bf16[192,1152]{1,0:T(8,128)(2,1)S(1)}, u32[]{:S(2)}, u32[]{:S(2)}) collective-permute-start(bf16[192,1152]{1,0:T(8,128)(2,1)S(1)} %collective-permute-done.3), channel_id=1, source_target_pairs={{16,24},{20,28},{17,25},{21,29},{18,26},{22,30},{19,27},{23,31}} | collective-permute-start | bytes 1327112 | tf_op jit(solution)/shard_map/ppermute | solution.py:719
  47.6 11.5 %collective-permute-start.6 = (bf16[192,1152]{1,0:T(8,128)(2,1)S(1)}, bf16[192,1152]{1,0:T(8,128)(2,1)}, u32[]{:S(2)}, u32[]{:S(2)}) collective-permute-start(bf16[192,1152]{1,0:T(8,128)(2,1)S(1)} %collective-permute-done.5), channel_id=1, source_target_pairs={{8,0},{12,4},{9,1},{13,5},{10,2},{14,6},{11,3},{15,7}} | collective-permute-start | bytes 1327112 | tf_op jit(solution)/shard_map/ppermute | solution.py:722
  59.1 371.0 %reduce-scatter.2.cloned.1.call-start = ((), (), s32[]{:S(2)}) async-start(), calls=%async_computation.6 | async-start | bytes 5308416 | tf_op jit(solution)/shard_map/reduce_scatter | solution.py:1044
  70.6 38.6 %collective-permute-start.7 = (bf16[576,1152]{1,0:T(8,128)(2,1)S(1)}, bf16[576,1152]{1,0:T(8,128)(2,1)S(1)}, u32[]{:S(2)}, u32[]{:S(2)}) collective-permute-start(bf16[576,1152]{1,0:T(8,128)(2,1)S(1)} %pad_maximum_fusion.2), channel_id=1, source_target_pairs={{0,4},{4,0},{8,12},{12,8},{16,20},{20,16},{24,28},{28,24},{1,5},{5... | collective-permute-start | bytes 3981320 | tf_op jit(solution)/shard_map/ppermute | solution.py:735
  205.1 22.4 %collective-permute-start.10 = (bf16[2,3,1024,384]{3,2,1,0:T(8,128)(2,1)}, bf16[2,3,1024,384]{3,2,1,0:T(8,128)(2,1)}, u32[]{:S(2)}, u32[]{:S(2)}) collective-permute-start(bf16[2,3,1024,384]{3,2,1,0:T(8,128)(2,1)} %get-tuple-element.103), channel_id=1, source_target_pairs={{0,1},{1,0},{2,3},{3,2},{4,5},{5,4},{6,7},{7,6},{8,9},{9,8},{10,11... | collective-permute-start | bytes 14155784 | tf_op jit(solution)/shard_map/ppermute | solution.py:1132
  231.6 63.3 %collective-permute-start.11 = (bf16[1024,384]{1,0:T(8,128)(2,1)}, bf16[1024,384]{1,0:T(8,128)(2,1)S(1)}, u32[]{:S(2)}, u32[]{:S(2)}) collective-permute-start(bf16[1024,384]{1,0:T(8,128)(2,1)} %get-tuple-element.121), channel_id=1, source_target_pairs={{0,2},{1,3},{2,0},{3,1},{4,6},{5,7},{6,4},{7,5},{8,10},{9,11},{10,... | collective-permute-start | bytes 2359304 | tf_op jit(solution)/shard_map/ppermute | solution.py:667
  233.1 61.9 %collective-permute-start.12 = (bf16[1024,384]{1,0:T(8,128)(2,1)}, bf16[1024,384]{1,0:T(8,128)(2,1)S(1)}, u32[]{:S(2)}, u32[]{:S(2)}) collective-permute-start(bf16[1024,384]{1,0:T(8,128)(2,1)} %get-tuple-element.122), channel_id=1, source_target_pairs={{0,2},{1,3},{2,0},{3,1},{4,6},{5,7},{6,4},{7,5},{8,10},{9,11},{10,... | collective-permute-start | bytes 2359304 | tf_op jit(solution)/shard_map/ppermute | solution.py:667
  233.6 61.3 %collective-permute-start.13 = (bf16[1024,384]{1,0:T(8,128)(2,1)}, bf16[1024,384]{1,0:T(8,128)(2,1)}, u32[]{:S(2)}, u32[]{:S(2)}) collective-permute-start(bf16[1024,384]{1,0:T(8,128)(2,1)} %get-tuple-element.123), channel_id=1, source_target_pairs={{0,2},{1,3},{2,0},{3,1},{4,6},{5,7},{6,4},{7,5},{8,10},{9,11},{10,... | collective-permute-start | bytes 2359304 | tf_op jit(solution)/shard_map/ppermute | solution.py:667
  294.9 13.3 %collective-permute-start.14 = (bf16[3,1024,256]{2,1,0:T(8,128)(2,1)}, bf16[3,1024,256]{2,1,0:T(8,128)(2,1)S(1)}, u32[]{:S(2)}, u32[]{:S(2)}) collective-permute-start(bf16[3,1024,256]{2,1,0:T(8,128)(2,1)} %get-tuple-element.129), channel_id=1, source_target_pairs={{0,1},{1,0},{2,3},{3,2},{4,5},{5,4},{6,7},{7,6},{8,9},{9,8},{10,11... | collective-permute-start | bytes 4718600 | tf_op jit(solution)/shard_map/ppermute | solution.py:754
  308.4 27.9 %collective-permute-start.15 = (bf16[3,512,256]{2,1,0:T(8,128)(2,1)S(1)}, bf16[3,512,256]{2,1,0:T(8,128)(2,1)S(1)}, u32[]{:S(2)}, u32[]{:S(2)}) collective-permute-start(bf16[3,512,256]{2,1,0:T(8,128)(2,1)S(1)} %add_convert_fusion.2), channel_id=1, source_target_pairs={{0,2},{1,3},{2,0},{3,1},{4,6},{5,7},{6,4},{7,5},{8,10},{9,11},{10,... | collective-permute-start | bytes 2359304 | tf_op jit(solution)/shard_map/ppermute | solution.py:764
  337.3 11.7 %collective-permute-start.16 = (bf16[2,3,1024,384]{3,2,1,0:T(8,128)(2,1)}, bf16[2,3,1024,384]{3,2,1,0:T(8,128)(2,1)}, u32[]{:S(2)}, u32[]{:S(2)}) collective-permute-start(bf16[2,3,1024,384]{3,2,1,0:T(8,128)(2,1)} %get-tuple-element.134), channel_id=1, source_target_pairs={{0,1},{1,0},{2,3},{3,2},{4,5},{5,4},{6,7},{7,6},{8,9},{9,8},{10,11... | collective-permute-start | bytes 14155784 | tf_op jit(solution)/shard_map/ppermute | solution.py:1180
  337.6 59.1 %all-to-all-start = ((bf16[8,192,768]{2,1,0:T(8,128)(2,1)}), bf16[8,192,768]{2,1,0:T(8,128)(2,1)}, u32[]{:S(2)}, u32[]{:S(2)}) async-start(bf16[8,192,768]{2,1,0:T(8,128)(2,1)} %bitcast.126), calls=%async_computation | async-start | bytes 4718592 | tf_op jit(solution)/shard_map/all_to_all | solution.py:1150
  414.5 32.7 %all-to-all-start.1 = ((bf16[8,192,384]{2,1,0:T(8,128)(2,1)}), bf16[8,192,384]{2,1,0:T(8,128)(2,1)}, u32[]{:S(2)}, u32[]{:S(2)}) async-start(bf16[8,192,384]{2,1,0:T(8,128)(2,1)} %bitcast.27), calls=%async_computation.2 | async-start | bytes 2359296 | tf_op jit(solution)/shard_map/all_to_all | solution.py:1210
  422.2 52.9 %collective-permute-start.18 = (bf16[3,1024,384]{2,1,0:T(8,128)(2,1)}, bf16[3,1024,384]{2,1,0:T(8,128)(2,1)}, u32[]{:S(2)}, u32[]{:S(2)}) collective-permute-start(bf16[3,1024,384]{2,1,0:T(8,128)(2,1)} %fusion.12), channel_id=1, source_target_pairs={{0,2},{1,3},{2,0},{3,1},{4,6},{5,7},{6,4},{7,5},{8,10},{9,11},{10,... | collective-permute-start | bytes 7077896 | tf_op jit(solution)/shard_map/ppermute | solution.py:667
  454.1 34.4 %all-to-all-start.2 = ((f32[24,64,128]{2,1,0:T(8,128)}), f32[24,64,128]{2,1,0:T(8,128)S(1)}, u32[]{:S(2)}, u32[]{:S(2)}) async-start(f32[24,64,128]{2,1,0:T(8,128)} %shard_map.313), calls=%async_computation.3 | async-start | bytes 1572864 | tf_op jit(solution)/shard_map/all_to_all | solution.py:814
  492.7 5.6 %collective-permute-start.21 = (f32[7460]{0:T(1024)S(1)}, f32[7460]{0:T(1024)S(1)}, u32[]{:S(2)}, u32[]{:S(2)}) collective-permute-start(f32[7460]{0:T(1024)S(1)} %concatenate.59), channel_id=1, source_target_pairs={{0,4},{4,0},{8,12},{12,8},{16,20},{20,16},{24,28},{28,24},{1,5},{5... | collective-permute-start | bytes 89528 | tf_op jit(solution)/shard_map/ppermute | solution.py:785
  498.3 6.1 %collective-permute-start.22 = (f32[7460]{0:T(1024)S(1)}, f32[7460]{0:T(1024)S(1)}, u32[]{:S(2)}, u32[]{:S(2)}) collective-permute-start(f32[7460]{0:T(1024)S(1)} %add.424), channel_id=1, source_target_pairs={{0,8},{4,12},{8,0},{12,4},{16,24},{20,28},{24,16},{28,20},{1,9},{5... | collective-permute-start | bytes 89528 | tf_op jit(solution)/shard_map/ppermute | solution.py:785
  500.7 21.3 %all-to-all-start.3 = ((bf16[8,3,64,128]{3,2,1,0:T(8,128)(2,1)}), bf16[8,3,64,128]{3,2,1,0:T(8,128)(2,1)S(1)}, u32[]{:S(2)}, u32[]{:S(2)}) async-start(bf16[8,3,64,128]{3,2,1,0:T(8,128)(2,1)} %broadcast_in_dim.57), calls=%async_computation.4 | async-start | bytes 786432 | tf_op jit(solution)/shard_map/all_to_all | solution.py:635
  504.4 12.0 %collective-permute-start.23 = (f32[7460]{0:T(1024)S(1)}, f32[7460]{0:T(1024)S(1)}, u32[]{:S(2)}, u32[]{:S(2)}) collective-permute-start(f32[7460]{0:T(1024)S(1)} %add.425), channel_id=1, source_target_pairs={{0,16},{4,20},{8,24},{12,28},{16,0},{20,4},{24,8},{28,12},{1,17},{... | collective-permute-start | bytes 89528 | tf_op jit(solution)/shard_map/ppermute | solution.py:785
  (31 other events, 449.4 us)
Sparse Core Ops, SparseCore 0:
  59.2 83.5 all-gather.1
  235.3 93.7 reduce-scatter.1
